TPU v7x, 32 devices: a whole 2x2x4 slice. The times are simulated.
32 devices in a mesh: groups: 2 (over x), dp: 16 (over z, y, core).
Axes of the slice: x: 2, y: 2, z: 4, core: 2. Of those that a mesh axis runs over, the one named last changes fastest.
Arguments:
- hidden_input_rows: bfloat16 [8192, 8192], P(('groups', 'dp')), parts along dimension 0, may hold values from -6 to 6
- rank_cotangent: bfloat16 [8192, 128], P(('groups', 'dp')), parts along dimension 0, may hold values from -0.25 to 0.25
- token_identifiers: int32 [8192], P(('groups', 'dp')), parts along dimension 0, may hold values from 0 to 31999, as said below
- adam_first_moment: float32 [8192, 128], P('dp'), may hold values from -0.6 to 0.6
- adam_second_moment: float32 [8192, 128], P('dp'), may hold values from 0.0001 to 0.01
- block_seeds: int32 [8], replicated, may hold values from 0 to 1073741823
Outputs:
- feature_rows: float32 [32, 2048], P(('groups', 'dp')), parts along dimension 0
There are 2 independent parts, one for each index of `groups`. A program takes and returns all parts, laid end to end along the dimension named above; an argument that names none is the same for every part. Nothing has to cross between parts.
Inputs may be any that keep to these rules, and one draw needn't show every extreme that they name: `token_identifiers`: 0 marks padding. In each sequence of 512 positions the real tokens (ids 1 and up) come first and number at least 128; the rest is padding. Some sequence has no padding.
All inputs are finite; a program needn't handle non-finite values.
Results may differ from a plain program's by a relative error of at most 0.0029.
Values sent between devices are 32-bit elements; how exact they have to be, the bound alone decides.
A program may use at most 64 MiB of HBM per device.

v0:
```python
import math

import jax
import jax.numpy as jnp
from jax import lax
from jax.sharding import PartitionSpec as P

FEAT_BLOCK = 512


beta_one = 0.9
beta_two = 0.999
epsilon = 1e-08
mix_feature = 1640531527
mix_param = 2028178513
mix_round = 73244475


def partner_2(value, axis, apart):
    mask = 2**apart
    pairs = [(source, source ^ mask) for source in range(lax.axis_size(axis))]
    return lax.ppermute(value, axis, pairs)


def scramble(hashed):
    hashed = hashed ^ lax.shift_right_logical(hashed, jnp.full_like(hashed, 16))
    hashed = hashed * mix_round
    hashed = hashed ^ lax.shift_right_logical(hashed, jnp.full_like(hashed, 16))
    hashed = hashed * mix_round
    hashed = hashed ^ lax.shift_right_logical(hashed, jnp.full_like(hashed, 16))
    return hashed


def sign_block(seed_values, feature_index, param_index):
    hashed = (
        seed_values[:, None]
        + feature_index[:, None] * mix_feature
        + param_index[None, :] * mix_param
    )
    hashed = scramble(hashed)
    return 1 - 2 * lax.shift_right_logical(hashed, jnp.full_like(hashed, 31))


def local(
    hidden_input_rows,
    rank_cotangent,
    token_identifiers,
    adam_first_moment,
    adam_second_moment,
    block_seeds,
):
    device_list = lax.axis_size("dp")
    my_index = lax.axis_index("dp")
    hidden_width = hidden_input_rows.shape[1]
    adapter_rank_size = rank_cotangent.shape[1]
    local_rows = adam_first_moment.shape[0]
    padding_mask = (token_identifiers != 0).astype(jnp.bfloat16)
    masked_values = rank_cotangent * padding_mask[:, None]
    half_gradient = lax.dot_general(
        hidden_input_rows,
        masked_values,
        (((0,), (0,)), ((), ())),
        preferred_element_type=jnp.float32,
    )
    block_list = half_gradient.reshape(device_list, local_rows, adapter_rank_size)
    half_rows = local_rows // 2
    split_blocks = block_list.reshape(device_list, 2, half_rows, adapter_rank_size)
    my_side = my_index % 2
    kept_rows = lax.dynamic_index_in_dim(split_blocks, my_side, 1, keepdims=False)
    given_rows = lax.dynamic_index_in_dim(split_blocks, 1 - my_side, 1, keepdims=False)
    partner = partner_2(given_rows, "dp", 0)
    summed = kept_rows + partner
    received_rows = lax.all_to_all(summed, "dp", split_axis=0, concat_axis=0, tiled=True)
    gradient = received_rows.reshape(device_list // 2, local_rows, adapter_rank_size)
    moment_one = beta_one * adam_first_moment[None] + (1 - beta_one) * gradient
    moment_two = beta_two * adam_second_moment[None] + (1 - beta_two) * gradient * gradient
    direction = (moment_one / (jnp.sqrt(moment_two) + epsilon)).astype(jnp.bfloat16)
    parameter_slice = local_rows * adapter_rank_size
    direction = direction.reshape(device_list // 2, parameter_slice)
    param_index = my_index * parameter_slice + jnp.arange(parameter_slice, dtype=jnp.int32)
    projection_scale = 1.0 / math.sqrt(hidden_width * adapter_rank_size)
    block_count = block_seeds.shape[0]

    def project(block_number, running):
        seed_value = lax.dynamic_index_in_dim(block_seeds, block_number, 0, keepdims=False)
        feature_index = block_number * FEAT_BLOCK + jnp.arange(FEAT_BLOCK, dtype=jnp.int32)
        seed_values = jnp.full((FEAT_BLOCK,), seed_value, jnp.int32)
        sign_tile = sign_block(seed_values, feature_index, param_index).astype(jnp.bfloat16)
        projected = lax.dot_general(
            direction, sign_tile, (((1,), (1,)), ((), ())), preferred_element_type=jnp.float32
        )
        return lax.dynamic_update_slice_in_dim(
            running, projected * projection_scale, block_number * FEAT_BLOCK, 1
        )

    partials = lax.fori_loop(
        jnp.int32(0),
        jnp.int32(block_count),
        project,
        jnp.zeros((device_list // 2, block_count * FEAT_BLOCK), jnp.float32),
    )
    partials = partials.reshape(device_list, block_count * FEAT_BLOCK // 2)
    return lax.psum_scatter(partials, "dp", scatter_dimension=0, tiled=True)


def solution(mesh):
    in_specs = (
        P(("groups", "dp"), None),
        P(("groups", "dp"), None),
        P(("groups", "dp")),
        P("dp", None),
        P("dp", None),
        P(),
    )
    out_specs = P(("groups", "dp"), None)
    return jax.shard_map(local, mesh=mesh, in_specs=in_specs, out_specs=out_specs, check_vma=False)
```

profile of v0, /device:TPU:0, one launch (start us, length us, event | category | flops | bytes accessed | tf_op | source)
XLA Modules:
  0.0 695.1 jit_solution(12888396023853559577)
XLA Ops:
  6.5 0.7 compare_convert_fusion
  7.2 5.0 convolution_bitcast_fusion
  12.2 6.6 reshape_reshape.3
  18.8 9.2 %constant_dynamic-slice_fusion.2 = (f32[16,1,256,128]{2,1,0,3:T(1,128)S(1)}, f32[16,1,256,128]{2,1,0,3:T(1,128)}) fusion(f32[16,2,256,128]{2,1,0,3:T(2,128)} %reshape_reshape.3, s32[]{:T(128)S(6)} %select_n.20, s32[]{:T(128)S(6)} %select_n.21), kind=kLoop, calls=%fused_computation.36 | loop fusion | bytes 8388616 | tf_op jit(solution)/shard_map/jit(dynamic_index_in_dim)/dynamic_slice | solution.py:69
  28.1 6.1 copy.12
  34.2 0.5 collective-permute-start
  34.6 3.8 copy.11
  38.5 0.3 collective-permute-done
  38.8 3.8 bitcast_add_fusion
  42.6 7.4 %all-to-all-start = ((f32[16,256,128]{2,1,0:T(8,128)}), f32[16,256,128]{2,1,0:T(8,128)}, u32[]{:S(2)}, u32[]{:S(2)}) async-start(f32[16,256,128]{2,1,0:T(8,128)} %bitcast_add_fusion), calls=%async_computation | async-start | bytes 4194304 | tf_op jit(solution)/shard_map/all_to_all | solution.py:73
  49.9 0.0 all-reduce.3.cloned.1.call-start
  50.0 0.0 copy-done
  50.0 0.0 copy-done.1
  50.1 0.0 copy-start.2
  50.1 41.0 %all-to-all-done = f32[16,256,128]{2,1,0:T(8,128)} async-done(((f32[16,256,128]{2,1,0:T(8,128)}), f32[16,256,128]{2,1,0:T(8,128)}, u32[]{:S(2)}, u32[]{:S(2)}) %all-to-all-start) | async-done | bytes 2097184 | tf_op jit(solution)/shard_map/all_to_all | solution.py:73
  91.1 2.0 reshape.29
  93.1 2.0 fusion.28
  95.1 0.0 copy-start.3
  95.1 496.8 %while.11 = (s32[]{:T(128)}, f32[8,4096]{1,0:T(8,128)S(1)}, s32[8]{0:T(128)S(1)}, bf16[8,65536]{1,0:T(8,128)(2,1)}, s32[]{:T(128)}, /*index=5*/s32[]{:T(128)}, s32[]{:T(128)}, s32[]{:T(128)}, s32[]{:T(128)}) while((s32[]{:T(128)}, f32[8,4096]{1,0:T(8,128)S(1)}, s32[8]{0:T(128)S(1)}, bf16[8,65536]{1,0:T(8,128)(2,1)}, s32[]{:T(128)}, ...), condition=%wide.region_1.2_spmd.clone, body=%wide.region_0.1_spmd.clone.sunk | while | flops 973215232 | bytes 1593511 | solution.py:96
  95.3 0.6 dynamic_slice.17
  96.0 0.6 multiply_add_fusion.2
  96.6 60.7 %fusion.41 = f32[8,4096]{1,0:T(8,128)S(1)} fusion(f32[8,4096]{1,0:T(8,128)S(1)} %get-tuple-element.101, s32[]{:T(128)S(6)} %select_n.24, bf16[8,65536]{1,0:T(8,128)(2,1)} %get-tuple-element.112, s32[65536]{0:T(1024)S(1)} %add_multiply_fusion.2, s32[512]{0:T(512)S(1)} %multiply_add_fusion.2), kind=kOutput, calls=%fused_computation.13.clone.2 | convolution fusion | flops 973082624 | bytes 1329156 | tf_op jit(solution)/shard_map/while/body/dot_general | solution.py:89
  157.4 0.6 dynamic_slice.17
  158.0 0.6 multiply_add_fusion.2
  158.7 60.7 %fusion.41 = f32[8,4096]{1,0:T(8,128)S(1)} fusion(f32[8,4096]{1,0:T(8,128)S(1)} %get-tuple-element.101, s32[]{:T(128)S(6)} %select_n.24, bf16[8,65536]{1,0:T(8,128)(2,1)} %get-tuple-element.112, s32[65536]{0:T(1024)S(1)} %add_multiply_fusion.2, s32[512]{0:T(512)S(1)} %multiply_add_fusion.2), kind=kOutput, calls=%fused_computation.13.clone.2 | convolution fusion | flops 973082624 | bytes 1329156 | tf_op jit(solution)/shard_map/while/body/dot_general | solution.py:89
  219.5 0.6 dynamic_slice.17
  220.1 0.6 multiply_add_fusion.2
  220.8 60.7 %fusion.41 = f32[8,4096]{1,0:T(8,128)S(1)} fusion(f32[8,4096]{1,0:T(8,128)S(1)} %get-tuple-element.101, s32[]{:T(128)S(6)} %select_n.24, bf16[8,65536]{1,0:T(8,128)(2,1)} %get-tuple-element.112, s32[65536]{0:T(1024)S(1)} %add_multiply_fusion.2, s32[512]{0:T(512)S(1)} %multiply_add_fusion.2), kind=kOutput, calls=%fused_computation.13.clone.2 | convolution fusion | flops 973082624 | bytes 1329156 | tf_op jit(solution)/shard_map/while/body/dot_general | solution.py:89
  281.5 0.6 dynamic_slice.17
  282.2 0.6 multiply_add_fusion.2
  282.9 60.7 %fusion.41 = f32[8,4096]{1,0:T(8,128)S(1)} fusion(f32[8,4096]{1,0:T(8,128)S(1)} %get-tuple-element.101, s32[]{:T(128)S(6)} %select_n.24, bf16[8,65536]{1,0:T(8,128)(2,1)} %get-tuple-element.112, s32[65536]{0:T(1024)S(1)} %add_multiply_fusion.2, s32[512]{0:T(512)S(1)} %multiply_add_fusion.2), kind=kOutput, calls=%fused_computation.13.clone.2 | convolution fusion | flops 973082624 | bytes 1329156 | tf_op jit(solution)/shard_map/while/body/dot_general | solution.py:89
  343.6 0.6 dynamic_slice.17
  344.3 0.6 multiply_add_fusion.2
  344.9 60.7 %fusion.41 = f32[8,4096]{1,0:T(8,128)S(1)} fusion(f32[8,4096]{1,0:T(8,128)S(1)} %get-tuple-element.101, s32[]{:T(128)S(6)} %select_n.24, bf16[8,65536]{1,0:T(8,128)(2,1)} %get-tuple-element.112, s32[65536]{0:T(1024)S(1)} %add_multiply_fusion.2, s32[512]{0:T(512)S(1)} %multiply_add_fusion.2), kind=kOutput, calls=%fused_computation.13.clone.2 | convolution fusion | flops 973082624 | bytes 1329156 | tf_op jit(solution)/shard_map/while/body/dot_general | solution.py:89
  405.7 0.6 dynamic_slice.17
  406.3 0.6 multiply_add_fusion.2
  407.0 60.7 %fusion.41 = f32[8,4096]{1,0:T(8,128)S(1)} fusion(f32[8,4096]{1,0:T(8,128)S(1)} %get-tuple-element.101, s32[]{:T(128)S(6)} %select_n.24, bf16[8,65536]{1,0:T(8,128)(2,1)} %get-tuple-element.112, s32[65536]{0:T(1024)S(1)} %add_multiply_fusion.2, s32[512]{0:T(512)S(1)} %multiply_add_fusion.2), kind=kOutput, calls=%fused_computation.13.clone.2 | convolution fusion | flops 973082624 | bytes 1329156 | tf_op jit(solution)/shard_map/while/body/dot_general | solution.py:89
  467.8 0.6 dynamic_slice.17
  468.4 0.6 multiply_add_fusion.2
  469.1 60.7 %fusion.41 = f32[8,4096]{1,0:T(8,128)S(1)} fusion(f32[8,4096]{1,0:T(8,128)S(1)} %get-tuple-element.101, s32[]{:T(128)S(6)} %select_n.24, bf16[8,65536]{1,0:T(8,128)(2,1)} %get-tuple-element.112, s32[65536]{0:T(1024)S(1)} %add_multiply_fusion.2, s32[512]{0:T(512)S(1)} %multiply_add_fusion.2), kind=kOutput, calls=%fused_computation.13.clone.2 | convolution fusion | flops 973082624 | bytes 1329156 | tf_op jit(solution)/shard_map/while/body/dot_general | solution.py:89
  529.8 0.6 dynamic_slice.17
  530.5 0.6 multiply_add_fusion.2
  531.2 60.7 %fusion.41 = f32[8,4096]{1,0:T(8,128)S(1)} fusion(f32[8,4096]{1,0:T(8,128)S(1)} %get-tuple-element.101, s32[]{:T(128)S(6)} %select_n.24, bf16[8,65536]{1,0:T(8,128)(2,1)} %get-tuple-element.112, s32[65536]{0:T(1024)S(1)} %add_multiply_fusion.2, s32[512]{0:T(512)S(1)} %multiply_add_fusion.2), kind=kOutput, calls=%fused_computation.13.clone.2 | convolution fusion | flops 973082624 | bytes 1329156 | tf_op jit(solution)/shard_map/while/body/dot_general | solution.py:89
  591.9 0.7 reshape.30
  592.6 0.0 all-reduce.3.cloned.1.call-update
  592.7 0.6 dynamic-slice
  593.3 93.0 %all-reduce.3.cloned.1.call-done = f32[16,2048]{1,0:T(8,128)} async-done(((f32[16,2048]{1,0:T(8,128)}), f32[16,2048]{1,0:T(8,128)}) %all-reduce.3.cloned.1.call-update) | async-done | bytes 131088
  686.3 2.0 constant_dynamic-slice_fusion
  (14 shorter events, 0.3 us)
Async XLA Ops:
  34.2 4.6 collective-permute-start
  38.5 11.5 %copy-start = (f32[512,128]{1,0:T(8,128)S(1)}, f32[512,128]{1,0:T(8,128)}, u32[]{:S(2)}) copy-start(f32[512,128]{1,0:T(8,128)} %param.12) | copy-start | bytes 786436
  38.5 11.5 %copy-start.1 = (f32[512,128]{1,0:T(8,128)S(1)}, f32[512,128]{1,0:T(8,128)}, u32[]{:S(2)}) copy-start(f32[512,128]{1,0:T(8,128)} %param.11) | copy-start | bytes 786436
  42.6 48.5 %all-to-all-start = ((f32[16,256,128]{2,1,0:T(8,128)}), f32[16,256,128]{2,1,0:T(8,128)}, u32[]{:S(2)}, u32[]{:S(2)}) async-start(f32[16,256,128]{2,1,0:T(8,128)} %bitcast_add_fusion), calls=%async_computation | async-start | bytes 4194304 | tf_op jit(solution)/shard_map/all_to_all | solution.py:73
  49.9 636.3 %all-reduce.3.cloned.1.call-start = ((), (), s32[]{:S(2)}) async-start(), calls=%async_computation.1 | async-start | bytes 262144
  50.1 45.1 %copy-start.2 = (s32[8]{0:T(128)S(1)}, s32[8]{0:T(128)}, u32[]{:S(2)}) copy-start(s32[8]{0:T(128)} %param.13) | copy-start | bytes 100
  95.1 497.6 %copy-start.3 = (u32[32]{0:T(128)S(1)}, u32[32]{0:T(128)}, u32[]{:S(2)}) copy-start(u32[32]{0:T(128)} %constant.74) | copy-start | bytes 388
Sparse Core Ops, SparseCore 0:
  592.8 93.4 all-reduce.2
where the time goes:
time: 697 us; the launch traced here: 695 us
  matrix products  491 us (70%)
  waiting for transfers between devices  134 us (19%)
  local copies, waits for them, and re-layouts  36.2 us (5%)
  between operations  13.5 us (2%)
  other arithmetic  11.9 us (2%)
  starting transfers between devices  7.86 us (1%)
    dot_general x8, matrix products, project(): lax.dot_general(direction, sign_tile, (((1,), (1,)), ((), ())), preferred...  486 us
    unnamed x2, waiting for transfers between devices  93 us
    all_to_all x1, waiting for transfers between devices, local(): lax.all_to_all(summed, 'dp', split_axis=0, concat_axis=0, tiled=True)  41 us
  transfers between devices with their start and end apart: 3, of which 3 were waited for; matrix products, arithmetic and copies ran while one was open for 1% of the time, Pallas kernels for 0%

commit v1 on v0

v1 whole, which is shorter than its diff:
```python
import functools
import math

import jax
import jax.numpy as jnp
from jax import lax
from jax.experimental import pallas as pl
from jax.experimental.pallas import tpu as pltpu
from jax.sharding import PartitionSpec as P

FEAT_BLOCK = 512


beta_one = 0.9
beta_two = 0.999
epsilon = 1e-08
mix_feature = 1640531527
mix_param = 2028178513
mix_round = 73244475

GRAD_COLUMNS = 1024
TILE_ROWS = 4
STRIP = 32


def wrapped(number):
    number %= 2**32
    return number - 2**32 if number >= 2**31 else number


def grad_kernel(shape, side_ref, hidden_ref, masked_ref, *out_refs):
    local_rows, groups, half, piece = shape
    chunks = half // piece
    product = lax.dot_general(
        hidden_ref[...],
        masked_ref[...],
        (((0,), (0,)), ((), ())),
        preferred_element_type=jnp.float32,
    )
    first = side_ref[0] == 0
    for owner in range(product.shape[0] // local_rows):
        for group in range(groups):
            start = owner * local_rows + group * 2 * half
            for chunk in range(chunks):
                low = start + chunk * piece
                low_rows = product[low : low + piece]
                high_rows = product[low + half : low + half + piece]
                out_refs[chunk][group, owner] = jnp.where(first, low_rows, high_rows)
                out_refs[chunks + chunk][group, owner] = jnp.where(first, high_rows, low_rows)


def half_gradients(hidden, masked, side, device_list, groups, half, piece):
    tokens, width = hidden.shape
    rank = masked.shape[1]
    local_rows = width // device_list
    chunks = half // piece
    owners = GRAD_COLUMNS // local_rows
    block = pl.BlockSpec((groups, owners, piece, rank), lambda step: (0, step, 0, 0))
    return pl.pallas_call(
        functools.partial(grad_kernel, (local_rows, groups, half, piece)),
        grid=(width // GRAD_COLUMNS,),
        in_specs=[
            pl.BlockSpec(memory_space=pltpu.SMEM),
            pl.BlockSpec((tokens, GRAD_COLUMNS), lambda step: (0, step)),
            pl.BlockSpec((tokens, rank), lambda step: (0, 0)),
        ],
        out_specs=[block] * (2 * chunks),
        out_shape=[jax.ShapeDtypeStruct((groups, device_list, piece, rank), jnp.float32)] * (2 * chunks),
        compiler_params=pltpu.CompilerParams(vmem_limit_bytes=32 * 2**20),
        cost_estimate=pl.CostEstimate(
            flops=2 * tokens * width * rank, bytes_accessed=2 * tokens * width + 4 * width * rank, transcendentals=0
        ),
    )(side, hidden, masked)


def sign_strip(hashed):
    hashed = hashed ^ lax.shift_right_logical(hashed, jnp.full_like(hashed, 16))
    hashed = hashed * mix_round
    hashed = hashed ^ lax.shift_right_logical(hashed, jnp.full_like(hashed, 16))
    hashed = hashed * mix_round
    return jnp.where(hashed < 0, -1.0, 1.0).astype(jnp.bfloat16)


def project_kernel(
    shape, place_ref, seeds_ref, grad_ref, one_ref, two_ref, before_ref, out_ref,
    directions, base, tile_a, tile_b, total,
):
    sequences, piece, half, rank, scale = shape
    block_number = pl.program_id(0)
    rows = 2 * piece
    tiles = rows // TILE_ROWS

    @pl.when(block_number == 0)
    def _():
        for side in range(2):
            def prepare(row, carry, side=side):
                gradient = grad_ref[pl.ds(side * piece + row, sequences, stride=rows), :]
                at = pl.ds(place_ref[0] + side * half + row, 1)
                moment_one = beta_one * one_ref[at, :] + (1 - beta_one) * gradient
                moment_two = beta_two * two_ref[at, :] + (1 - beta_two) * gradient * gradient
                direction = moment_one / (jnp.sqrt(moment_two) + epsilon)
                directions[side * piece + row] = direction.astype(jnp.bfloat16)
                return carry

            lax.fori_loop(0, piece, prepare, 0)

    feature = block_number * FEAT_BLOCK + lax.broadcasted_iota(jnp.int32, base.shape, 0)
    column = lax.broadcasted_iota(jnp.int32, base.shape, 1)
    base[...] = seeds_ref[block_number] + feature * mix_feature + column * mix_param
    total[...] = jnp.zeros_like(total)
    row_step = jnp.int32(wrapped(mix_param * rank))

    def fill(tile, held):
        row = tile * TILE_ROWS
        side = row // piece
        first = place_ref[1] + side * half + (row - side * piece)
        for step in range(TILE_ROWS):
            offset = (first + step) * row_step
            for strip in range(0, FEAT_BLOCK, STRIP):
                held[strip : strip + STRIP, step * rank : (step + 1) * rank] = sign_strip(
                    base[strip : strip + STRIP, :] + offset
                )

    def add(tile, held):
        weights = jnp.concatenate(
            [directions[tile * TILE_ROWS + step] for step in range(TILE_ROWS)], axis=1
        )
        total[...] += lax.dot_general(
            held[...], weights, (((1,), (1,)), ((), ())), preferred_element_type=jnp.float32
        )

    fill(0, tile_a)

    def pair(index, carry):
        add(2 * index, tile_a)
        fill(2 * index + 1, tile_b)
        add(2 * index + 1, tile_b)
        fill(2 * index + 2, tile_a)
        return carry

    lax.fori_loop(0, tiles // 2 - 1, pair, 0)
    add(tiles - 2, tile_a)
    fill(tiles - 1, tile_b)
    add(tiles - 1, tile_b)
    out_ref[...] = before_ref[...] + total[...].T * scale


def project(place, seeds, received, moment_one, moment_two, before, sequences, piece, half, scale):
    rank = received.shape[1]
    features = seeds.shape[0] * FEAT_BLOCK
    rows = 2 * piece
    whole = lambda array: pl.BlockSpec(array.shape, lambda block: (0, 0))
    part = pl.BlockSpec((sequences, FEAT_BLOCK), lambda block: (0, block))
    return pl.pallas_call(
        functools.partial(project_kernel, (sequences, piece, half, rank, scale)),
        grid=(seeds.shape[0],),
        in_specs=[
            pl.BlockSpec(memory_space=pltpu.SMEM),
            pl.BlockSpec(memory_space=pltpu.SMEM),
            whole(received),
            whole(moment_one),
            whole(moment_two),
            part,
        ],
        out_specs=part,
        out_shape=jax.ShapeDtypeStruct((sequences, features), jnp.float32),
        scratch_shapes=[
            pltpu.VMEM((rows, sequences, rank), jnp.bfloat16),
            pltpu.VMEM((FEAT_BLOCK, rank), jnp.int32),
            pltpu.VMEM((FEAT_BLOCK, TILE_ROWS * rank), jnp.bfloat16),
            pltpu.VMEM((FEAT_BLOCK, TILE_ROWS * rank), jnp.bfloat16),
            pltpu.VMEM((FEAT_BLOCK, sequences), jnp.float32),
        ],
        compiler_params=pltpu.CompilerParams(vmem_limit_bytes=32 * 2**20),
        cost_estimate=pl.CostEstimate(
            flops=400 * rows * rank * features, bytes_accessed=4 * received.size, transcendentals=0
        ),
    )(place, seeds, received, moment_one, moment_two, before)


def local(
    hidden_input_rows,
    rank_cotangent,
    token_identifiers,
    adam_first_moment,
    adam_second_moment,
    block_seeds,
):
    axes = ("groups", "dp")
    groups = lax.axis_size("groups")
    device_list = lax.axis_size("dp")
    my_group = lax.axis_index("groups")
    my_index = lax.axis_index("dp")
    hidden_width = hidden_input_rows.shape[1]
    rank = rank_cotangent.shape[1]
    local_rows = adam_first_moment.shape[0]
    owned = local_rows // groups
    half = owned // 2
    piece = max(8, half // 4)
    devices = groups * device_list
    sequences = devices // 2
    scale = 1.0 / math.sqrt(hidden_width * rank)

    padding_mask = (token_identifiers != 0).astype(jnp.bfloat16)
    masked_values = rank_cotangent * padding_mask[:, None]
    side = jnp.reshape(my_index % 2, (1,)).astype(jnp.int32)
    blocks = half_gradients(hidden_input_rows, masked_values, side, device_list, groups, half, piece)
    chunks = half // piece
    pairs = [(source, source ^ 1) for source in range(device_list)]
    received = []
    for chunk in range(chunks):
        other = lax.ppermute(blocks[chunks + chunk], "dp", pairs)
        summed = (blocks[chunk] + other).reshape(devices, piece, rank)
        gathered = lax.all_to_all(summed, axes, split_axis=0, concat_axis=0, tiled=True)
        received.append(gathered.reshape(devices * piece, rank))

    partials = jnp.zeros((sequences, block_seeds.shape[0] * FEAT_BLOCK), jnp.float32)
    for chunk in range(chunks):
        in_slice = my_group * owned + chunk * piece
        place = jnp.stack([in_slice, my_index * local_rows + in_slice]).astype(jnp.int32)
        partials = project(
            place, block_seeds, received[chunk], adam_first_moment, adam_second_moment, partials,
            sequences, piece, half, scale,
        )
    shares = partials.reshape(devices, -1)
    shares = lax.all_to_all(shares, axes, split_axis=0, concat_axis=0, tiled=True)
    return jnp.sum(shares, axis=0, keepdims=True)


def solution(mesh):
    in_specs = (
        P(("groups", "dp"), None),
        P(("groups", "dp"), None),
        P(("groups", "dp")),
        P("dp", None),
        P("dp", None),
        P(),
    )
    out_specs = P(("groups", "dp"), None)
    return jax.shard_map(local, mesh=mesh, in_specs=in_specs, out_specs=out_specs, check_vma=False)
```

time: 697 us -> 329 us (0.47)
  matrix products: 491 us -> 0 us
  Pallas kernels: 0 us -> 267 us
  waiting for transfers between devices: 134 us -> 10.4 us
  local copies, waits for them, and re-layouts: 36.2 us -> 2.55 us
  blocking collectives: 0 us -> 15.9 us
  starting transfers between devices: 7.86 us -> 22.8 us
  between operations: 13.5 us -> 0.14 us
    dot_general x9 -> x0, matrix products: 491 us -> none  [the longest x8 486 us: project(): lax.dot_general(direction, sign_tile, (((1,), (1,)), ((), ())), preferred...]
    pallas_call x0 -> x5, Pallas kernels: none -> 267 us  [the longest x4 263 us: project(): pl.pallas_call(functools.partial(project_kernel, (sequences, piece, half,...]
    unnamed x2 -> x0, waiting for transfers between devices: 93 us -> none
    all_to_all x1 -> x4, waiting for transfers between devices: 41 us -> 7.65 us  [local(): lax.all_to_all(summed, axes, split_axis=0, concat_axis=0, tiled=True)]
    all_to_all x0 -> x1, blocking collectives: none -> 15.9 us  [local(): lax.all_to_all(shares, axes, split_axis=0, concat_axis=0, tiled=True)]
    dynamic_slice x9 -> x0, local copies, waits for them, and re-layouts: 14.3 us -> none  [the longest x1 9.24 us: local(): lax.dynamic_index_in_dim(split_blocks, my_side, 1, keepdims=False)]
    all_to_all x1 -> x4, starting transfers between devices: 7.36 us -> 21.5 us  [local(): lax.all_to_all(summed, axes, split_axis=0, concat_axis=0, tiled=True)]
    unnamed x12 -> x10, local copies, waits for them, and re-layouts: 12.6 us -> 2.2 us
  transfers between devices with their start and end apart: 3 -> 8, of which waited for: 3 -> 3; matrix products, arithmetic and copies ran while one was open for 1% -> 2% of each run, Pallas kernels for 0% -> 60%
where the time goes in v1:
time: 329 us; the launch traced here: 328 us
  Pallas kernels  267 us (81%)
  starting transfers between devices  22.8 us (7%)
  blocking collectives  15.9 us (5%)
  waiting for transfers between devices  10.4 us (3%)
  other arithmetic  9.49 us (3%)
    pallas_call x4, Pallas kernels, project(): pl.pallas_call(functools.partial(project_kernel, (sequences, piece, half,...  263 us
    all_to_all x4, starting transfers between devices, local(): lax.all_to_all(summed, axes, split_axis=0, concat_axis=0, tiled=True)  21.5 us
    all_to_all x1, blocking collectives, local(): lax.all_to_all(shares, axes, split_axis=0, concat_axis=0, tiled=True)  15.9 us
    all_to_all x4, waiting for transfers between devices, local(): lax.all_to_all(summed, axes, split_axis=0, concat_axis=0, tiled=True)  7.65 us
    add x4, other arithmetic, local(): summed = (blocks[chunk] + other).reshape(devices, piece, rank)  6.81 us
  transfers between devices with their start and end apart: 8, of which 3 were waited for; matrix products, arithmetic and copies ran while one was open for 2% of the time, Pallas kernels for 60%

profile of v1, /device:TPU:0, one launch (start us, length us, event | category | flops | bytes accessed | tf_op | source)
XLA Modules:
  0.0 328.1 jit_solution(8154073251583518574)
XLA Ops:
  0.0 0.7 compare_convert_fusion
  0.7 0.9 broadcast_multiply_fusion.masked_ref
  1.6 0.0 copy-start
  1.6 2.2 copy-done
  3.8 3.5 %shard_map.64 = (f32[2,16,32,128]{3,2,1,0:T(8,128)S(1)}, f32[2,16,32,128]{3,2,1,0:T(8,128)S(1)}, f32[2,16,32,128]{3,2,1,0:T(8,128)S(1)}, f32[2,16,32,128]{3,2,1,...) custom-call(s32[1]{0:T(128)} %bitcast.2.side_ref, ...), custom_call_target="tpu_custom_call" | custom-call | flops 536870912 | bytes 8388608 | tf_op jit(solution)/shard_map/pallas_call | solution.py:59
  7.4 0.0 copy-start.1
  7.4 0.5 collective-permute-start.3
  7.9 1.5 collective-permute-done.3
  9.4 0.0 copy-start.2
  9.4 0.0 copy-start.4
  9.4 0.9 add.48
  10.3 0.0 copy-done.1
  10.3 7.2 %all-to-all-start.3 = ((f32[32,32,128]{2,1,0:T(8,128)}), f32[32,32,128]{2,1,0:T(8,128)S(1)}, u32[]{:S(2)}, u32[]{:S(2)}) async-start(f32[32,32,128]{2,1,0:T(8,128)} %bitcast.22), calls=%async_computation.3 | async-start | bytes 1048576 | tf_op jit(solution)/shard_map/all_to_all | solution.py:214
  17.5 0.3 collective-permute-start.2
  17.8 0.3 collective-permute-start.1
  18.1 0.3 collective-permute-start
  18.4 0.1 pad_add_fusion.3.place_ref
  18.4 0.1 pad_add_fusion.2.place_ref
  18.5 0.1 pad_add_fusion.1.place_ref
  18.6 0.1 pad_add_fusion.place_ref
  18.7 1.2 collective-permute-done.2
  19.8 2.0 add.46
  21.8 0.0 copy-start.3
  21.8 0.0 collective-permute-done.1
  21.8 2.0 add.43
  23.8 0.0 collective-permute-done
  23.8 2.0 add.40
  25.8 7.6 %all-to-all-done.3 = f32[32,32,128]{2,1,0:T(8,128)S(1)} async-done(((f32[32,32,128]{2,1,0:T(8,128)}), f32[32,32,128]{2,1,0:T(8,128)S(1)}, u32[]{:S(2)}, u32[]{:S(2)}) %all-to-all-start.3) | async-done | bytes 524320 | tf_op jit(solution)/shard_map/all_to_all | solution.py:214
  33.4 2.6 all-to-all-start.2
  36.1 0.0 copy-done.2
  36.1 0.0 copy-done.4
  36.1 0.0 copy-done.3
  36.1 65.8 %shard_map.65.before_ref = f32[16,4096]{1,0:T(8,128)S(1)} custom-call(s32[2]{0:T(128)S(1)} %pad_add_fusion.3.place_ref, s32[8]{0:T(128)S(1)} %copy-done.4, f32[1024,128]{1,0:T(8,128)S(1)} %bitcast.18, f32[512,128]{1,0:T(8,128)S(1)} %copy-done.2, f32[512,128]{1,0:T(8,128)S(1)} %copy-done.3, f32[16,4096]{1,0:T(8,128)S(1)} %broadcast_in_dim.7.before_ref), custom_call_target="tpu_custom_call" | custom-call | flops 13421772800 | bytes 524288 | tf_op jit(solution)/shard_map/pallas_call | solution.py:154
  101.9 0.0 all-to-all-done.2
  101.9 5.8 %all-to-all-start.1 = ((f32[32,32,128]{2,1,0:T(8,128)}), f32[32,32,128]{2,1,0:T(8,128)S(1)}, u32[]{:S(2)}, u32[]{:S(2)}) async-start(f32[32,32,128]{2,1,0:T(8,128)} %bitcast.7), calls=%async_computation.1 | async-start | bytes 1048576 | tf_op jit(solution)/shard_map/all_to_all | solution.py:214
  107.8 65.8 %shard_map.66.before_ref = f32[16,4096]{1,0:T(8,128)S(1)} custom-call(s32[2]{0:T(128)S(1)} %pad_add_fusion.2.place_ref, s32[8]{0:T(128)S(1)} %copy-done.4, f32[1024,128]{1,0:T(8,128)S(1)} %bitcast.19, f32[512,128]{1,0:T(8,128)S(1)} %copy-done.2, f32[512,128]{1,0:T(8,128)S(1)} %copy-done.3, f32[16,4096]{1,0:T(8,128)S(1)} %shard_map.65.before_ref), custom_call_target="tpu_custom_call" | custom-call | flops 13421772800 | bytes 524288 | tf_op jit(solution)/shard_map/pallas_call | solution.py:154
  173.6 0.0 all-to-all-done.1
  173.6 5.8 %all-to-all-start = ((f32[32,32,128]{2,1,0:T(8,128)}), f32[32,32,128]{2,1,0:T(8,128)S(1)}, u32[]{:S(2)}, u32[]{:S(2)}) async-start(f32[32,32,128]{2,1,0:T(8,128)} %bitcast.3), calls=%async_computation | async-start | bytes 1048576 | tf_op jit(solution)/shard_map/all_to_all | solution.py:214
  179.4 65.8 %shard_map.67.before_ref = f32[16,4096]{1,0:T(8,128)S(1)} custom-call(s32[2]{0:T(128)S(1)} %pad_add_fusion.1.place_ref, s32[8]{0:T(128)S(1)} %copy-done.4, f32[1024,128]{1,0:T(8,128)S(1)} %bitcast.20, f32[512,128]{1,0:T(8,128)S(1)} %copy-done.2, f32[512,128]{1,0:T(8,128)S(1)} %copy-done.3, f32[16,4096]{1,0:T(8,128)S(1)} %shard_map.66.before_ref), custom_call_target="tpu_custom_call" | custom-call | flops 13421772800 | bytes 524288 | tf_op jit(solution)/shard_map/pallas_call | solution.py:154
  245.2 0.0 all-to-all-done
  245.3 65.8 %shard_map.68 = f32[16,4096]{1,0:T(8,128)S(1)} custom-call(s32[2]{0:T(128)S(1)} %pad_add_fusion.place_ref, s32[8]{0:T(128)S(1)} %copy-done.4, f32[1024,128]{1,0:T(8,128)S(1)} %bitcast.21, f32[512,128]{1,0:T(8,128)S(1)} %copy-done.2, f32[512,128]{1,0:T(8,128)S(1)} %copy-done.3, f32[16,4096]{1,0:T(8,128)S(1)} %shard_map.67.before_ref), custom_call_target="tpu_custom_call" | custom-call | flops 13421772800 | bytes 524288 | tf_op jit(solution)/shard_map/pallas_call | solution.py:154
  311.1 0.3 all_to_all.24
  311.4 15.9 %all_to_all.30 = f32[32,1,2048]{2,1,0:T(1,128)S(1)} all-to-all(f32[32,1,2048]{2,1,0:T(1,128)S(1)} %all_to_all.24), channel_id=1, replica_groups=mesh['groups'=2,'dp'=16] {'groups','dp'}, dimensions={0} | all-to-all | bytes 524288 | tf_op jit(solution)/shard_map/all_to_all | solution.py:226
  327.3 0.8 reduce_sum.9
  (1 shorter events, 0.0 us)
Async XLA Ops:
  1.6 2.2 copy-start
  7.4 2.9 copy-start.1
  7.4 2.1 collective-permute-start.3
  9.4 26.7 %copy-start.2 = (f32[512,128]{1,0:T(8,128)S(1)}, f32[512,128]{1,0:T(8,128)}, u32[]{:S(2)}) copy-start(f32[512,128]{1,0:T(8,128)} %one_ref.7) | copy-start | bytes 786436
  9.4 26.7 %copy-start.4 = (s32[8]{0:T(128)S(1)}, s32[8]{0:T(128)}, u32[]{:S(2)}) copy-start(s32[8]{0:T(128)} %seeds_ref.7) | copy-start | bytes 100
  10.3 23.1 %all-to-all-start.3 = ((f32[32,32,128]{2,1,0:T(8,128)}), f32[32,32,128]{2,1,0:T(8,128)S(1)}, u32[]{:S(2)}, u32[]{:S(2)}) async-start(f32[32,32,128]{2,1,0:T(8,128)} %bitcast.22), calls=%async_computation.3 | async-start | bytes 1048576 | tf_op jit(solution)/shard_map/all_to_all | solution.py:214
  17.5 2.3 collective-permute-start.2
  17.8 4.0 %collective-permute-start.1 = (f32[2,16,32,128]{3,2,1,0:T(8,128)S(1)}, f32[2,16,32,128]{3,2,1,0:T(8,128)}, u32[]{:S(2)}, u32[]{:S(2)}) collective-permute-start(f32[2,16,32,128]{3,2,1,0:T(8,128)S(1)} %get-tuple-element.16), channel_id=1, source_target_pairs={{0,1},{1,0},{2,3},{3,2},{4,5},{5,4},{6,7},{7,6},{8,9},{9,8},{10,11... | collective-permute-start | bytes 1572872 | tf_op jit(solution)/shard_map/ppermute | solution.py:212
  18.1 5.7 %collective-permute-start = (f32[2,16,32,128]{3,2,1,0:T(8,128)S(1)}, f32[2,16,32,128]{3,2,1,0:T(8,128)}, u32[]{:S(2)}, u32[]{:S(2)}) collective-permute-start(f32[2,16,32,128]{3,2,1,0:T(8,128)S(1)} %get-tuple-element.14), channel_id=1, source_target_pairs={{0,1},{1,0},{2,3},{3,2},{4,5},{5,4},{6,7},{7,6},{8,9},{9,8},{10,11... | collective-permute-start | bytes 1572872 | tf_op jit(solution)/shard_map/ppermute | solution.py:212
  21.8 14.3 %copy-start.3 = (f32[512,128]{1,0:T(8,128)S(1)}, f32[512,128]{1,0:T(8,128)}, u32[]{:S(2)}) copy-start(f32[512,128]{1,0:T(8,128)} %two_ref.7) | copy-start | bytes 786436
  33.4 68.5 %all-to-all-start.2 = ((f32[32,32,128]{2,1,0:T(8,128)}), f32[32,32,128]{2,1,0:T(8,128)S(1)}, u32[]{:S(2)}, u32[]{:S(2)}) async-start(f32[32,32,128]{2,1,0:T(8,128)} %bitcast.23), calls=%async_computation.2 | async-start | bytes 1048576 | tf_op jit(solution)/shard_map/all_to_all | solution.py:214
  101.9 71.7 %all-to-all-start.1 = ((f32[32,32,128]{2,1,0:T(8,128)}), f32[32,32,128]{2,1,0:T(8,128)S(1)}, u32[]{:S(2)}, u32[]{:S(2)}) async-start(f32[32,32,128]{2,1,0:T(8,128)} %bitcast.7), calls=%async_computation.1 | async-start | bytes 1048576 | tf_op jit(solution)/shard_map/all_to_all | solution.py:214
  173.6 71.7 %all-to-all-start = ((f32[32,32,128]{2,1,0:T(8,128)}), f32[32,32,128]{2,1,0:T(8,128)S(1)}, u32[]{:S(2)}, u32[]{:S(2)}) async-start(f32[32,32,128]{2,1,0:T(8,128)} %bitcast.3), calls=%async_computation | async-start | bytes 1048576 | tf_op jit(solution)/shard_map/all_to_all | solution.py:214

commit v2 on v1

--- a/solution.py
+++ b/solution.py
@@ -20,7 +20,7 @@
 
 GRAD_COLUMNS = 1024
 TILE_ROWS = 4
-STRIP = 32
+STRIP = 16
 
 
 def wrapped(number):
@@ -29,8 +29,8 @@
 
 
 def grad_kernel(shape, side_ref, hidden_ref, masked_ref, *out_refs):
-    local_rows, groups, half, piece = shape
-    chunks = half // piece
+    local_rows, groups, half, pieces = shape
+    chunks = len(pieces)
     product = lax.dot_general(
         hidden_ref[...],
         masked_ref[...],
@@ -41,31 +41,34 @@
     for owner in range(product.shape[0] // local_rows):
         for group in range(groups):
             start = owner * local_rows + group * 2 * half
-            for chunk in range(chunks):
-                low = start + chunk * piece
+            for chunk, (offset, piece) in enumerate(pieces):
+                low = start + offset
                 low_rows = product[low : low + piece]
                 high_rows = product[low + half : low + half + piece]
                 out_refs[chunk][group, owner] = jnp.where(first, low_rows, high_rows)
                 out_refs[chunks + chunk][group, owner] = jnp.where(first, high_rows, low_rows)
 
 
-def half_gradients(hidden, masked, side, device_list, groups, half, piece):
+def half_gradients(hidden, masked, side, device_list, groups, half, pieces):
     tokens, width = hidden.shape
     rank = masked.shape[1]
     local_rows = width // device_list
-    chunks = half // piece
+    sizes = [piece for _, piece in pieces] * 2
     owners = GRAD_COLUMNS // local_rows
-    block = pl.BlockSpec((groups, owners, piece, rank), lambda step: (0, step, 0, 0))
     return pl.pallas_call(
-        functools.partial(grad_kernel, (local_rows, groups, half, piece)),
+        functools.partial(grad_kernel, (local_rows, groups, half, pieces)),
         grid=(width // GRAD_COLUMNS,),
         in_specs=[
             pl.BlockSpec(memory_space=pltpu.SMEM),
             pl.BlockSpec((tokens, GRAD_COLUMNS), lambda step: (0, step)),
             pl.BlockSpec((tokens, rank), lambda step: (0, 0)),
         ],
-        out_specs=[block] * (2 * chunks),
-        out_shape=[jax.ShapeDtypeStruct((groups, device_list, piece, rank), jnp.float32)] * (2 * chunks),
+        out_specs=[
+            pl.BlockSpec((groups, owners, size, rank), lambda step: (0, step, 0, 0)) for size in sizes
+        ],
+        out_shape=[
+            jax.ShapeDtypeStruct((groups, device_list, size, rank), jnp.float32) for size in sizes
+        ],
         compiler_params=pltpu.CompilerParams(vmem_limit_bytes=32 * 2**20),
         cost_estimate=pl.CostEstimate(
             flops=2 * tokens * width * rank, bytes_accessed=2 * tokens * width + 4 * width * rank, transcendentals=0
@@ -104,8 +107,8 @@
 
             lax.fori_loop(0, piece, prepare, 0)
 
-    feature = block_number * FEAT_BLOCK + lax.broadcasted_iota(jnp.int32, base.shape, 0)
-    column = lax.broadcasted_iota(jnp.int32, base.shape, 1)
+    column = lax.broadcasted_iota(jnp.int32, base.shape, 0)
+    feature = block_number * FEAT_BLOCK + lax.broadcasted_iota(jnp.int32, base.shape, 1)
     base[...] = seeds_ref[block_number] + feature * mix_feature + column * mix_param
     total[...] = jnp.zeros_like(total)
     row_step = jnp.int32(wrapped(mix_param * rank))
@@ -116,18 +119,15 @@
         first = place_ref[1] + side * half + (row - side * piece)
         for step in range(TILE_ROWS):
             offset = (first + step) * row_step
-            for strip in range(0, FEAT_BLOCK, STRIP):
-                held[strip : strip + STRIP, step * rank : (step + 1) * rank] = sign_strip(
-                    base[strip : strip + STRIP, :] + offset
-                )
+            for strip in range(0, rank, STRIP):
+                at = step * rank + strip
+                held[at : at + STRIP, :] = sign_strip(base[strip : strip + STRIP, :] + offset)
 
     def add(tile, held):
-        weights = jnp.concatenate(
+        directed = jnp.concatenate(
             [directions[tile * TILE_ROWS + step] for step in range(TILE_ROWS)], axis=1
         )
-        total[...] += lax.dot_general(
-            held[...], weights, (((1,), (1,)), ((), ())), preferred_element_type=jnp.float32
-        )
+        total[...] += jnp.dot(directed, held[...], preferred_element_type=jnp.float32)
 
     fill(0, tile_a)
 
@@ -142,7 +142,7 @@
     add(tiles - 2, tile_a)
     fill(tiles - 1, tile_b)
     add(tiles - 1, tile_b)
-    out_ref[...] = before_ref[...] + total[...].T * scale
+    out_ref[...] = before_ref[...] + total[...] * scale
 
 
 def project(place, seeds, received, moment_one, moment_two, before, sequences, piece, half, scale):
@@ -166,10 +166,10 @@
         out_shape=jax.ShapeDtypeStruct((sequences, features), jnp.float32),
         scratch_shapes=[
             pltpu.VMEM((rows, sequences, rank), jnp.bfloat16),
-            pltpu.VMEM((FEAT_BLOCK, rank), jnp.int32),
-            pltpu.VMEM((FEAT_BLOCK, TILE_ROWS * rank), jnp.bfloat16),
-            pltpu.VMEM((FEAT_BLOCK, TILE_ROWS * rank), jnp.bfloat16),
-            pltpu.VMEM((FEAT_BLOCK, sequences), jnp.float32),
+            pltpu.VMEM((rank, FEAT_BLOCK), jnp.int32),
+            pltpu.VMEM((TILE_ROWS * rank, FEAT_BLOCK), jnp.bfloat16),
+            pltpu.VMEM((TILE_ROWS * rank, FEAT_BLOCK), jnp.bfloat16),
+            pltpu.VMEM((sequences, FEAT_BLOCK), jnp.float32),
         ],
         compiler_params=pltpu.CompilerParams(vmem_limit_bytes=32 * 2**20),
         cost_estimate=pl.CostEstimate(
@@ -196,7 +196,8 @@
     local_rows = adam_first_moment.shape[0]
     owned = local_rows // groups
     half = owned // 2
-    piece = max(8, half // 4)
+    first = max(8, half // 4)
+    pieces = ((0, first), (first, half - first))
     devices = groups * device_list
     sequences = devices // 2
     scale = 1.0 / math.sqrt(hidden_width * rank)
@@ -204,19 +205,19 @@
     padding_mask = (token_identifiers != 0).astype(jnp.bfloat16)
     masked_values = rank_cotangent * padding_mask[:, None]
     side = jnp.reshape(my_index % 2, (1,)).astype(jnp.int32)
-    blocks = half_gradients(hidden_input_rows, masked_values, side, device_list, groups, half, piece)
-    chunks = half // piece
+    blocks = half_gradients(hidden_input_rows, masked_values, side, device_list, groups, half, pieces)
+    chunks = len(pieces)
     pairs = [(source, source ^ 1) for source in range(device_list)]
     received = []
-    for chunk in range(chunks):
+    for chunk, (_, piece) in enumerate(pieces):
         other = lax.ppermute(blocks[chunks + chunk], "dp", pairs)
         summed = (blocks[chunk] + other).reshape(devices, piece, rank)
         gathered = lax.all_to_all(summed, axes, split_axis=0, concat_axis=0, tiled=True)
         received.append(gathered.reshape(devices * piece, rank))
 
     partials = jnp.zeros((sequences, block_seeds.shape[0] * FEAT_BLOCK), jnp.float32)
-    for chunk in range(chunks):
-        in_slice = my_group * owned + chunk * piece
+    for chunk, (offset, piece) in enumerate(pieces):
+        in_slice = my_group * owned + offset
         place = jnp.stack([in_slice, my_index * local_rows + in_slice]).astype(jnp.int32)
         partials = project(
             place, block_seeds, received[chunk], adam_first_moment, adam_second_moment, partials,

time: 329 us -> 268 us (0.81)
  Pallas kernels: 267 us -> 216 us
  starting transfers between devices: 22.8 us -> 10.3 us
  waiting for transfers between devices: 10.4 us -> 16.8 us
  other arithmetic: 9.49 us -> 6.16 us
    pallas_call x4 -> x2, Pallas kernels: 263 us -> 211 us  [project(): pl.pallas_call(functools.partial(project_kernel, (sequences, piece, half,...]
    all_to_all x4 -> x2, starting transfers between devices: 21.5 us -> 9.76 us  [local(): lax.all_to_all(summed, axes, split_axis=0, concat_axis=0, tiled=True)]
    all_to_all x4 -> x2, waiting for transfers between devices: 7.65 us -> 13.1 us  [local(): lax.all_to_all(summed, axes, split_axis=0, concat_axis=0, tiled=True)]
    add x4 -> x2, other arithmetic: 6.81 us -> 3.63 us  [local(): summed = (blocks[chunk] + other).reshape(devices, piece, rank)]
  transfers between devices with their start and end apart: 8 -> 4, of which waited for: 3 -> 2; matrix products, arithmetic and copies ran while one was open for 2% -> 1% of each run, Pallas kernels for 60% -> 20%
where the time goes in v2:
time: 268 us
  Pallas kernels  216 us (81%)
  waiting for transfers between devices  16.8 us (6%)
  blocking collectives  15.9 us (6%)
  starting transfers between devices  10.3 us (4%)
  other arithmetic  6.16 us (2%)
    pallas_call x2, Pallas kernels, project(): pl.pallas_call(functools.partial(project_kernel, (sequences, piece, half,...  211 us
    all_to_all x1, blocking collectives, local(): lax.all_to_all(shares, axes, split_axis=0, concat_axis=0, tiled=True)  15.9 us
    all_to_all x2, waiting for transfers between devices, local(): lax.all_to_all(summed, axes, split_axis=0, concat_axis=0, tiled=True)  13.1 us
    all_to_all x2, starting transfers between devices, local(): lax.all_to_all(summed, axes, split_axis=0, concat_axis=0, tiled=True)  9.76 us
  transfers between devices with their start and end apart: 4, of which 2 were waited for; matrix products, arithmetic and copies ran while one was open for 1% of the time, Pallas kernels for 20%

profile of v2, /device:TPU:0, one launch (start us, length us, event | category | flops | bytes accessed | tf_op | source)
XLA Modules:
  0.0 267.8 jit_solution(6734408997636889987)
XLA Ops:
  0.0 0.7 compare_convert_fusion
  0.7 0.9 broadcast_multiply_fusion.masked_ref
  1.6 0.0 copy-start
  1.6 2.2 copy-done
  3.8 4.8 %shard_map.64 = (f32[2,16,32,128]{3,2,1,0:T(8,128)S(1)}, f32[2,16,96,128]{3,2,1,0:T(8,128)S(1)}, f32[2,16,32,128]{3,2,1,0:T(8,128)S(1)}, f32[2,16,96,128]{3,2,1,0:T(8,128)}) custom-call(s32[1]{0:T(128)} %bitcast.2.side_ref, bf16[256,8192]{1,0:T(8,128)(2,1)S(1)} %copy-done, bf16[256,128]{1,0:T(8,128)(2,1)S(1)} %broadcast_multiply_fusion.masked_ref), custom_call_target="tpu_custom_call" | custom-call | flops 536870912 | bytes 8388608 | tf_op jit(solution)/shard_map/pallas_call | solution.py:58
  8.6 0.5 collective-permute-start
  9.0 0.1 collective-permute-start.1
  9.1 3.6 %collective-permute-done.1 = f32[2,16,32,128]{3,2,1,0:T(8,128)S(1)} collective-permute-done((f32[2,16,32,128]{3,2,1,0:T(8,128)S(1)}, f32[2,16,32,128]{3,2,1,0:T(8,128)S(1)}, u32[]{:S(2)}, u32[]{:S(2)}) %collective-permute-start.1) | collective-permute-done | bytes 524320 | tf_op jit(solution)/shard_map/ppermute | solution.py:213
  12.7 0.9 add.24
  13.6 6.9 %all-to-all-start.1 = ((f32[32,32,128]{2,1,0:T(8,128)}), f32[32,32,128]{2,1,0:T(8,128)S(1)}, u32[]{:S(2)}, u32[]{:S(2)}) async-start(f32[32,32,128]{2,1,0:T(8,128)} %bitcast.7), calls=%async_computation.1 | async-start | bytes 1048576 | tf_op jit(solution)/shard_map/all_to_all | solution.py:215
  20.6 0.0 collective-permute-done
  20.6 2.7 %add.22 = f32[2,16,96,128]{3,2,1,0:T(8,128)} add(f32[2,16,96,128]{3,2,1,0:T(8,128)S(1)} %get-tuple-element.9, f32[2,16,96,128]{3,2,1,0:T(8,128)} %collective-permute-done) | non-fusion elementwise | flops 393216 | bytes 4718592 | tf_op jit(solution)/shard_map/add | solution.py:214
  23.3 13.1 %all-to-all-done.1 = f32[32,32,128]{2,1,0:T(8,128)S(1)} async-done(((f32[32,32,128]{2,1,0:T(8,128)}), f32[32,32,128]{2,1,0:T(8,128)S(1)}, u32[]{:S(2)}, u32[]{:S(2)}) %all-to-all-start.1) | async-done | bytes 524320 | tf_op jit(solution)/shard_map/all_to_all | solution.py:215
  36.5 0.0 copy-start.1
  36.5 0.0 copy-start.2
  36.5 0.0 copy-start.3
  36.5 2.8 %all-to-all-start = ((f32[32,96,128]{2,1,0:T(8,128)}), f32[32,96,128]{2,1,0:T(8,128)S(1)}, u32[]{:S(2)}, u32[]{:S(2)}) async-start(f32[32,96,128]{2,1,0:T(8,128)} %bitcast.12), calls=%async_computation | async-start | bytes 3145728 | tf_op jit(solution)/shard_map/all_to_all | solution.py:215
  39.3 0.1 pad_add_fusion.place_ref
  39.4 0.1 pad_add_fusion.1.place_ref
  39.5 0.0 copy-done.1
  39.5 0.0 copy-done.2
  39.5 0.0 copy-done.3
  39.5 53.3 %shard_map.65.before_ref = f32[16,4096]{1,0:T(8,128)S(1)} custom-call(s32[2]{0:T(128)S(1)} %pad_add_fusion.1.place_ref, s32[8]{0:T(128)S(1)} %copy-done.3, f32[1024,128]{1,0:T(8,128)S(1)} %bitcast.11, f32[512,128]{1,0:T(8,128)S(1)} %copy-done.1, f32[512,128]{1,0:T(8,128)S(1)} %copy-done.2, f32[16,4096]{1,0:T(8,128)S(1)} %broadcast_in_dim.7.before_ref), custom_call_target="tpu_custom_call" | custom-call | flops 13421772800 | bytes 524288 | tf_op jit(solution)/shard_map/pallas_call | solution.py:154
  92.8 0.0 all-to-all-done
  92.8 157.9 %shard_map.66 = f32[16,4096]{1,0:T(8,128)S(1)} custom-call(s32[2]{0:T(128)S(1)} %pad_add_fusion.place_ref, s32[8]{0:T(128)S(1)} %copy-done.3, f32[3072,128]{1,0:T(8,128)S(1)} %bitcast.10, f32[512,128]{1,0:T(8,128)S(1)} %copy-done.1, f32[512,128]{1,0:T(8,128)S(1)} %copy-done.2, f32[16,4096]{1,0:T(8,128)S(1)} %shard_map.65.before_ref), custom_call_target="tpu_custom_call" | custom-call | flops 40265318400 | bytes 1572864 | tf_op jit(solution)/shard_map/pallas_call | solution.py:154
  250.7 0.3 all_to_all.16
  251.1 15.9 %all_to_all.20 = f32[32,1,2048]{2,1,0:T(1,128)S(1)} all-to-all(f32[32,1,2048]{2,1,0:T(1,128)S(1)} %all_to_all.16), channel_id=1, replica_groups=mesh['groups'=2,'dp'=16] {'groups','dp'}, dimensions={0} | all-to-all | bytes 524288 | tf_op jit(solution)/shard_map/all_to_all | solution.py:227
  267.0 0.8 reduce_sum.9
  (1 shorter events, 0.0 us)
Async XLA Ops:
  1.6 2.2 copy-start
  8.6 12.0 %collective-permute-start = (f32[2,16,96,128]{3,2,1,0:T(8,128)}, f32[2,16,96,128]{3,2,1,0:T(8,128)}, u32[]{:S(2)}, u32[]{:S(2)}) collective-permute-start(f32[2,16,96,128]{3,2,1,0:T(8,128)} %get-tuple-element.10), channel_id=1, source_target_pairs={{0,1},{1,0},{2,3},{3,2},{4,5},{5,4},{6,7},{7,6},{8,9},{9,8},{10,11... | collective-permute-start | bytes 4718600 | tf_op jit(solution)/shard_map/ppermute | solution.py:213
  9.0 3.7 %collective-permute-start.1 = (f32[2,16,32,128]{3,2,1,0:T(8,128)S(1)}, f32[2,16,32,128]{3,2,1,0:T(8,128)S(1)}, u32[]{:S(2)}, u32[]{:S(2)}) collective-permute-start(f32[2,16,32,128]{3,2,1,0:T(8,128)S(1)} %get-tuple-element.12), channel_id=1, source_target_pairs={{0,1},{1,0},{2,3},{3,2},{4,5},{5,4},{6,7},{7,6},{8,9},{9,8},{10,11... | collective-permute-start | bytes 1572872 | tf_op jit(solution)/shard_map/ppermute | solution.py:213
  13.6 22.9 %all-to-all-start.1 = ((f32[32,32,128]{2,1,0:T(8,128)}), f32[32,32,128]{2,1,0:T(8,128)S(1)}, u32[]{:S(2)}, u32[]{:S(2)}) async-start(f32[32,32,128]{2,1,0:T(8,128)} %bitcast.7), calls=%async_computation.1 | async-start | bytes 1048576 | tf_op jit(solution)/shard_map/all_to_all | solution.py:215
  36.5 3.0 %copy-start.1 = (f32[512,128]{1,0:T(8,128)S(1)}, f32[512,128]{1,0:T(8,128)}, u32[]{:S(2)}) copy-start(f32[512,128]{1,0:T(8,128)} %one_ref.3) | copy-start | bytes 786436
  36.5 3.0 %copy-start.2 = (f32[512,128]{1,0:T(8,128)S(1)}, f32[512,128]{1,0:T(8,128)}, u32[]{:S(2)}) copy-start(f32[512,128]{1,0:T(8,128)} %two_ref.3) | copy-start | bytes 786436
  36.5 3.0 %copy-start.3 = (s32[8]{0:T(128)S(1)}, s32[8]{0:T(128)}, u32[]{:S(2)}) copy-start(s32[8]{0:T(128)} %seeds_ref.3) | copy-start | bytes 100
  36.5 56.3 %all-to-all-start = ((f32[32,96,128]{2,1,0:T(8,128)}), f32[32,96,128]{2,1,0:T(8,128)S(1)}, u32[]{:S(2)}, u32[]{:S(2)}) async-start(f32[32,96,128]{2,1,0:T(8,128)} %bitcast.12), calls=%async_computation | async-start | bytes 3145728 | tf_op jit(solution)/shard_map/all_to_all | solution.py:215

commit v3 on v2

--- a/solution.py
+++ b/solution.py
@@ -19,8 +19,9 @@
 mix_round = 73244475
 
 GRAD_COLUMNS = 1024
-TILE_ROWS = 4
+TILE_ROWS = 2
 STRIP = 16
+PASS_COLUMNS = 256
 
 
 def wrapped(number):
@@ -113,35 +114,44 @@
     total[...] = jnp.zeros_like(total)
     row_step = jnp.int32(wrapped(mix_param * rank))
 
-    def fill(tile, held):
+    passes = FEAT_BLOCK // PASS_COLUMNS
+    strips = [
+        (step, strip) for step in range(TILE_ROWS) for strip in range(0, rank, STRIP)
+    ]
+
+    def fill(tile, held, part):
         row = tile * TILE_ROWS
         side = row // piece
         first = place_ref[1] + side * half + (row - side * piece)
-        for step in range(TILE_ROWS):
+        for step, strip in strips[part * len(strips) // passes : (part + 1) * len(strips) // passes]:
+            at = step * rank + strip
             offset = (first + step) * row_step
-            for strip in range(0, rank, STRIP):
-                at = step * rank + strip
-                held[at : at + STRIP, :] = sign_strip(base[strip : strip + STRIP, :] + offset)
-
-    def add(tile, held):
+            held[at : at + STRIP, :] = sign_strip(base[strip : strip + STRIP, :] + offset)
+
+    def add(tile, held, part):
         directed = jnp.concatenate(
             [directions[tile * TILE_ROWS + step] for step in range(TILE_ROWS)], axis=1
         )
-        total[...] += jnp.dot(directed, held[...], preferred_element_type=jnp.float32)
-
-    fill(0, tile_a)
+        columns = pl.ds(part * PASS_COLUMNS, PASS_COLUMNS)
+        total[:, columns] += jnp.dot(directed, held[:, columns], preferred_element_type=jnp.float32)
+
+    def both(tile, held, other):
+        for part in range(passes):
+            add(tile, held, part)
+            fill(tile + 1, other, part)
+
+    for part in range(passes):
+        fill(0, tile_a, part)
 
     def pair(index, carry):
-        add(2 * index, tile_a)
-        fill(2 * index + 1, tile_b)
-        add(2 * index + 1, tile_b)
-        fill(2 * index + 2, tile_a)
+        both(2 * index, tile_a, tile_b)
+        both(2 * index + 1, tile_b, tile_a)
         return carry
 
     lax.fori_loop(0, tiles // 2 - 1, pair, 0)
-    add(tiles - 2, tile_a)
-    fill(tiles - 1, tile_b)
-    add(tiles - 1, tile_b)
+    both(tiles - 2, tile_a, tile_b)
+    for part in range(passes):
+        add(tiles - 1, tile_b, part)
     out_ref[...] = before_ref[...] + total[...] * scale
 
 
@@ -176,6 +186,61 @@
             flops=400 * rows * rank * features, bytes_accessed=4 * received.size, transcendentals=0
         ),
     )(place, seeds, received, moment_one, moment_two, before)
+
+
+def gather_kernel(groups, device_list, shares_ref, out_ref, landing, send_sem, recv_sem):
+    devices = groups * device_list
+    me = lax.axis_index("groups") * device_list + lax.axis_index("dp")
+
+    def place(offset):
+        target = lax.rem(me + offset, devices)
+        return target, (target // device_list, lax.rem(target, device_list))
+
+    barrier = pltpu.get_barrier_semaphore()
+
+    def greet(offset, carry):
+        pl.semaphore_signal(barrier, inc=1, device_id=place(offset)[1], device_id_type=pl.DeviceIdType.MESH)
+        return carry
+
+    lax.fori_loop(1, devices, greet, 0)
+    pl.semaphore_wait(barrier, devices - 1)
+
+    def send(offset, carry):
+        target, where = place(offset)
+        pltpu.make_async_remote_copy(
+            src_ref=shares_ref.at[target],
+            dst_ref=landing.at[offset - 1],
+            send_sem=send_sem,
+            recv_sem=recv_sem,
+            device_id=where,
+            device_id_type=pl.DeviceIdType.MESH,
+        ).start()
+        return carry
+
+    lax.fori_loop(1, devices, send, 0)
+    pltpu.make_async_copy(landing, landing, recv_sem).wait()
+    out_ref[...] = shares_ref[me] + jnp.sum(landing[...], axis=0)
+    pltpu.make_async_copy(landing, landing, send_sem).wait()
+
+
+def sum_shares(shares, groups, device_list):
+    devices, rows, columns = shares.shape
+    vmem = pl.BlockSpec(memory_space=pltpu.VMEM)
+    return pl.pallas_call(
+        functools.partial(gather_kernel, groups, device_list),
+        in_specs=[vmem],
+        out_specs=vmem,
+        out_shape=jax.ShapeDtypeStruct((rows, columns), jnp.float32),
+        scratch_shapes=[
+            pltpu.VMEM((devices - 1, rows, columns), jnp.float32),
+            pltpu.SemaphoreType.DMA,
+            pltpu.SemaphoreType.DMA,
+        ],
+        compiler_params=pltpu.CompilerParams(
+            collective_id=0, has_side_effects=True, vmem_limit_bytes=32 * 2**20
+        ),
+        cost_estimate=pl.CostEstimate(flops=shares.size, bytes_accessed=8 * shares.size, transcendentals=0),
+    )(shares)
 
 
 def local(
@@ -223,9 +288,8 @@
             place, block_seeds, received[chunk], adam_first_moment, adam_second_moment, partials,
             sequences, piece, half, scale,
         )
-    shares = partials.reshape(devices, -1)
-    shares = lax.all_to_all(shares, axes, split_axis=0, concat_axis=0, tiled=True)
-    return jnp.sum(shares, axis=0, keepdims=True)
+    shares = partials.reshape(devices, 8, -1)
+    return sum_shares(shares, groups, device_list).reshape(1, -1)
 
 
 def solution(mesh):

time: 268 us -> 298 us (1.11)
  Pallas kernels: 216 us -> 263 us
  blocking collectives: 15.9 us -> 0 us
    pallas_call x2, Pallas kernels: 211 us -> 246 us  [project(): pl.pallas_call(functools.partial(project_kernel, (sequences, piece, half,...]
    all_to_all x1 -> x0, blocking collectives: 15.9 us -> none  [local(): lax.all_to_all(shares, axes, split_axis=0, concat_axis=0, tiled=True)]
    pallas_call x0 -> x1, Pallas kernels: none -> 12 us  [sum_shares(): pl.pallas_call(functools.partial(gather_kernel, groups, device_list), in_...]
  transfers between devices with their start and end apart: 4 -> 4, of which waited for: 2 -> 2; matrix products, arithmetic and copies ran while one was open for 1% -> 1% of each run, Pallas kernels for 20% -> 21%
where the time goes in v3:
time: 298 us
  Pallas kernels  263 us (88%)
  waiting for transfers between devices  16.8 us (6%)
  starting transfers between devices  10.3 us (3%)
  other arithmetic  5.41 us (2%)
    pallas_call x2, Pallas kernels, project(): pl.pallas_call(functools.partial(project_kernel, (sequences, piece, half,...  246 us
    all_to_all x2, waiting for transfers between devices, local(): lax.all_to_all(summed, axes, split_axis=0, concat_axis=0, tiled=True)  13.1 us
    pallas_call x1, Pallas kernels, sum_shares(): pl.pallas_call(functools.partial(gather_kernel, groups, device_list), in_...  12 us
    all_to_all x2, starting transfers between devices, local(): lax.all_to_all(summed, axes, split_axis=0, concat_axis=0, tiled=True)  9.76 us
  transfers between devices with their start and end apart: 4, of which 2 were waited for; matrix products, arithmetic and copies ran while one was open for 1% of the time, Pallas kernels for 21%

profile of v3, /device:TPU:0, one launch (start us, length us, event | category | flops | bytes accessed | tf_op | source)
XLA Modules:
  0.0 298.1 jit_solution(14454520823892212031)
XLA Ops:
  0.0 0.7 compare_convert_fusion
  0.7 0.9 broadcast_multiply_fusion.masked_ref
  1.6 0.0 copy-start
  1.6 2.2 copy-done
  3.8 4.8 %shard_map.64 = (f32[2,16,32,128]{3,2,1,0:T(8,128)S(1)}, f32[2,16,96,128]{3,2,1,0:T(8,128)S(1)}, f32[2,16,32,128]{3,2,1,0:T(8,128)S(1)}, f32[2,16,96,128]{3,2,1,0:T(8,128)}) custom-call(s32[1]{0:T(128)} %bitcast.2.side_ref, bf16[256,8192]{1,0:T(8,128)(2,1)S(1)} %copy-done, bf16[256,128]{1,0:T(8,128)(2,1)S(1)} %broadcast_multiply_fusion.masked_ref), custom_call_target="tpu_custom_call" | custom-call | flops 536870912 | bytes 8388608 | tf_op jit(solution)/shard_map/pallas_call | solution.py:59
  8.6 0.5 collective-permute-start
  9.1 0.1 collective-permute-start.1
  9.1 3.6 %collective-permute-done.1 = f32[2,16,32,128]{3,2,1,0:T(8,128)S(1)} collective-permute-done((f32[2,16,32,128]{3,2,1,0:T(8,128)S(1)}, f32[2,16,32,128]{3,2,1,0:T(8,128)S(1)}, u32[]{:S(2)}, u32[]{:S(2)}) %collective-permute-start.1) | collective-permute-done | bytes 524320 | tf_op jit(solution)/shard_map/ppermute | solution.py:278
  12.8 0.9 add.24
  13.7 6.9 %all-to-all-start.1 = ((f32[32,32,128]{2,1,0:T(8,128)}), f32[32,32,128]{2,1,0:T(8,128)S(1)}, u32[]{:S(2)}, u32[]{:S(2)}) async-start(f32[32,32,128]{2,1,0:T(8,128)} %bitcast.7), calls=%async_computation.1 | async-start | bytes 1048576 | tf_op jit(solution)/shard_map/all_to_all | solution.py:280
  20.6 0.0 collective-permute-done
  20.6 2.8 add.22
  23.4 13.1 %all-to-all-done.1 = f32[32,32,128]{2,1,0:T(8,128)S(1)} async-done(((f32[32,32,128]{2,1,0:T(8,128)}), f32[32,32,128]{2,1,0:T(8,128)S(1)}, u32[]{:S(2)}, u32[]{:S(2)}) %all-to-all-start.1) | async-done | bytes 524320 | tf_op jit(solution)/shard_map/all_to_all | solution.py:280
  36.5 0.0 copy-start.1
  36.5 0.0 copy-start.2
  36.5 0.0 copy-start.3
  36.5 2.8 all-to-all-start
  39.4 0.1 pad_add_fusion.place_ref
  39.5 0.1 pad_add_fusion.1.place_ref
  39.5 0.0 copy-done.1
  39.6 0.0 copy-done.2
  39.6 0.0 copy-done.3
  39.6 61.7 %shard_map.65.before_ref = f32[16,4096]{1,0:T(8,128)S(1)} custom-call(s32[2]{0:T(128)S(1)} %pad_add_fusion.1.place_ref, s32[8]{0:T(128)S(1)} %copy-done.3, f32[1024,128]{1,0:T(8,128)S(1)} %bitcast.13, f32[512,128]{1,0:T(8,128)S(1)} %copy-done.1, f32[512,128]{1,0:T(8,128)S(1)} %copy-done.2, f32[16,4096]{1,0:T(8,128)S(1)} %broadcast_in_dim.4.before_ref), custom_call_target="tpu_custom_call" | custom-call | flops 13421772800 | bytes 524288 | tf_op jit(solution)/shard_map/pallas_call | solution.py:164
  101.2 0.0 all-to-all-done
  101.3 184.2 %shard_map.66 = f32[16,4096]{1,0:T(8,128)S(1)} custom-call(s32[2]{0:T(128)S(1)} %pad_add_fusion.place_ref, s32[8]{0:T(128)S(1)} %copy-done.3, f32[3072,128]{1,0:T(8,128)S(1)} %bitcast.12, f32[512,128]{1,0:T(8,128)S(1)} %copy-done.1, f32[512,128]{1,0:T(8,128)S(1)} %copy-done.2, f32[16,4096]{1,0:T(8,128)S(1)} %shard_map.65.before_ref), custom_call_target="tpu_custom_call" | custom-call | flops 40265318400 | bytes 1572864 | tf_op jit(solution)/shard_map/pallas_call | solution.py:164
  285.5 12.0 %shard_map.67 = f32[8,256]{1,0:T(8,128)S(1)} custom-call(f32[32,8,256]{2,1,0:T(8,128)S(1)} %reshape.27.shares_ref), custom_call_target="tpu_custom_call" | custom-call | flops 65536 | bytes 524288 | tf_op jit(solution)/shard_map/pallas_call | solution.py:229
  297.5 0.6 copy.7
  (2 shorter events, 0.1 us)
Async XLA Ops:
  1.6 2.2 copy-start
  8.6 12.0 %collective-permute-start = (f32[2,16,96,128]{3,2,1,0:T(8,128)}, f32[2,16,96,128]{3,2,1,0:T(8,128)}, u32[]{:S(2)}, u32[]{:S(2)}) collective-permute-start(f32[2,16,96,128]{3,2,1,0:T(8,128)} %get-tuple-element.10), channel_id=1, source_target_pairs={{0,1},{1,0},{2,3},{3,2},{4,5},{5,4},{6,7},{7,6},{8,9},{9,8},{10,11... | collective-permute-start | bytes 4718600 | tf_op jit(solution)/shard_map/ppermute | solution.py:278
  9.1 3.7 %collective-permute-start.1 = (f32[2,16,32,128]{3,2,1,0:T(8,128)S(1)}, f32[2,16,32,128]{3,2,1,0:T(8,128)S(1)}, u32[]{:S(2)}, u32[]{:S(2)}) collective-permute-start(f32[2,16,32,128]{3,2,1,0:T(8,128)S(1)} %get-tuple-element.12), channel_id=1, source_target_pairs={{0,1},{1,0},{2,3},{3,2},{4,5},{5,4},{6,7},{7,6},{8,9},{9,8},{10,11... | collective-permute-start | bytes 1572872 | tf_op jit(solution)/shard_map/ppermute | solution.py:278
  13.7 22.9 %all-to-all-start.1 = ((f32[32,32,128]{2,1,0:T(8,128)}), f32[32,32,128]{2,1,0:T(8,128)S(1)}, u32[]{:S(2)}, u32[]{:S(2)}) async-start(f32[32,32,128]{2,1,0:T(8,128)} %bitcast.7), calls=%async_computation.1 | async-start | bytes 1048576 | tf_op jit(solution)/shard_map/all_to_all | solution.py:280
  36.5 3.0 %copy-start.1 = (f32[512,128]{1,0:T(8,128)S(1)}, f32[512,128]{1,0:T(8,128)}, u32[]{:S(2)}) copy-start(f32[512,128]{1,0:T(8,128)} %one_ref.3) | copy-start | bytes 786436
  36.5 3.0 %copy-start.2 = (f32[512,128]{1,0:T(8,128)S(1)}, f32[512,128]{1,0:T(8,128)}, u32[]{:S(2)}) copy-start(f32[512,128]{1,0:T(8,128)} %two_ref.3) | copy-start | bytes 786436
  36.5 3.0 %copy-start.3 = (s32[8]{0:T(128)S(1)}, s32[8]{0:T(128)}, u32[]{:S(2)}) copy-start(s32[8]{0:T(128)} %seeds_ref.3) | copy-start | bytes 100
  36.5 64.7 %all-to-all-start = ((f32[32,96,128]{2,1,0:T(8,128)}), f32[32,96,128]{2,1,0:T(8,128)S(1)}, u32[]{:S(2)}, u32[]{:S(2)}) async-start(f32[32,96,128]{2,1,0:T(8,128)} %bitcast.15), calls=%async_computation | async-start | bytes 3145728 | tf_op jit(solution)/shard_map/all_to_all | solution.py:280

commit v4 on v3

--- a/solution.py
+++ b/solution.py
@@ -20,7 +20,8 @@
 
 GRAD_COLUMNS = 1024
 TILE_ROWS = 2
-STRIP = 16
+BODY_ROWS = 16
+STRIP = 32
 PASS_COLUMNS = 256
 
 
@@ -87,12 +88,11 @@
 
 def project_kernel(
     shape, place_ref, seeds_ref, grad_ref, one_ref, two_ref, before_ref, out_ref,
-    directions, base, tile_a, tile_b, total,
+    directions, base,
 ):
     sequences, piece, half, rank, scale = shape
     block_number = pl.program_id(0)
     rows = 2 * piece
-    tiles = rows // TILE_ROWS
 
     @pl.when(block_number == 0)
     def _():
@@ -111,48 +111,35 @@
     column = lax.broadcasted_iota(jnp.int32, base.shape, 0)
     feature = block_number * FEAT_BLOCK + lax.broadcasted_iota(jnp.int32, base.shape, 1)
     base[...] = seeds_ref[block_number] + feature * mix_feature + column * mix_param
-    total[...] = jnp.zeros_like(total)
     row_step = jnp.int32(wrapped(mix_param * rank))
 
     passes = FEAT_BLOCK // PASS_COLUMNS
-    strips = [
-        (step, strip) for step in range(TILE_ROWS) for strip in range(0, rank, STRIP)
-    ]
-
-    def fill(tile, held, part):
-        row = tile * TILE_ROWS
-        side = row // piece
-        first = place_ref[1] + side * half + (row - side * piece)
-        for step, strip in strips[part * len(strips) // passes : (part + 1) * len(strips) // passes]:
-            at = step * rank + strip
-            offset = (first + step) * row_step
-            held[at : at + STRIP, :] = sign_strip(base[strip : strip + STRIP, :] + offset)
-
-    def add(tile, held, part):
-        directed = jnp.concatenate(
-            [directions[tile * TILE_ROWS + step] for step in range(TILE_ROWS)], axis=1
-        )
-        columns = pl.ds(part * PASS_COLUMNS, PASS_COLUMNS)
-        total[:, columns] += jnp.dot(directed, held[:, columns], preferred_element_type=jnp.float32)
-
-    def both(tile, held, other):
-        for part in range(passes):
-            add(tile, held, part)
-            fill(tile + 1, other, part)
-
-    for part in range(passes):
-        fill(0, tile_a, part)
-
-    def pair(index, carry):
-        both(2 * index, tile_a, tile_b)
-        both(2 * index + 1, tile_b, tile_a)
-        return carry
-
-    lax.fori_loop(0, tiles // 2 - 1, pair, 0)
-    both(tiles - 2, tile_a, tile_b)
-    for part in range(passes):
-        add(tiles - 1, tile_b, part)
-    out_ref[...] = before_ref[...] + total[...] * scale
+
+    def body(index, sums):
+        sums = list(sums)
+        for tile in range(BODY_ROWS // TILE_ROWS):
+            row = index * BODY_ROWS + tile * TILE_ROWS
+            side = row // piece
+            first = place_ref[1] + side * half + (row - side * piece)
+            directed = jnp.concatenate(
+                [directions[row + step] for step in range(TILE_ROWS)], axis=1
+            )
+            for part in range(passes):
+                columns = slice(part * PASS_COLUMNS, (part + 1) * PASS_COLUMNS)
+                signs = jnp.concatenate(
+                    [
+                        sign_strip(base[strip : strip + STRIP, columns] + (first + step) * row_step)
+                        for step in range(TILE_ROWS)
+                        for strip in range(0, rank, STRIP)
+                    ],
+                    axis=0,
+                )
+                sums[part] += jnp.dot(directed, signs, preferred_element_type=jnp.float32)
+        return tuple(sums)
+
+    zero = jnp.zeros((sequences, PASS_COLUMNS), jnp.float32)
+    sums = lax.fori_loop(0, rows // BODY_ROWS, body, (zero,) * passes)
+    out_ref[...] = before_ref[...] + jnp.concatenate(sums, axis=1) * scale
 
 
 def project(place, seeds, received, moment_one, moment_two, before, sequences, piece, half, scale):
@@ -177,9 +164,6 @@
         scratch_shapes=[
             pltpu.VMEM((rows, sequences, rank), jnp.bfloat16),
             pltpu.VMEM((rank, FEAT_BLOCK), jnp.int32),
-            pltpu.VMEM((TILE_ROWS * rank, FEAT_BLOCK), jnp.bfloat16),
-            pltpu.VMEM((TILE_ROWS * rank, FEAT_BLOCK), jnp.bfloat16),
-            pltpu.VMEM((sequences, FEAT_BLOCK), jnp.float32),
         ],
         compiler_params=pltpu.CompilerParams(vmem_limit_bytes=32 * 2**20),
         cost_estimate=pl.CostEstimate(

time: 298 us -> 243 us (0.82)
  Pallas kernels: 263 us -> 207 us
    pallas_call x2, Pallas kernels: 246 us -> 190 us  [project(): pl.pallas_call(functools.partial(project_kernel, (sequences, piece, half,...]
  transfers between devices with their start and end apart: 4 -> 4, of which waited for: 2 -> 2; matrix products, arithmetic and copies ran while one was open for 1% -> 2% of each run, Pallas kernels for 21% -> 20%
where the time goes in v4:
time: 243 us
  Pallas kernels  207 us (85%)
  waiting for transfers between devices  16.8 us (7%)
  starting transfers between devices  10.3 us (4%)
  other arithmetic  5.41 us (2%)
  local copies, waits for them, and re-layouts  2.87 us (1%)
    pallas_call x2, Pallas kernels, project(): pl.pallas_call(functools.partial(project_kernel, (sequences, piece, half,...  190 us
    all_to_all x2, waiting for transfers between devices, local(): lax.all_to_all(summed, axes, split_axis=0, concat_axis=0, tiled=True)  13.1 us
    pallas_call x1, Pallas kernels, sum_shares(): pl.pallas_call(functools.partial(gather_kernel, groups, device_list), in_...  12 us
    all_to_all x2, starting transfers between devices, local(): lax.all_to_all(summed, axes, split_axis=0, concat_axis=0, tiled=True)  9.76 us
  transfers between devices with their start and end apart: 4, of which 2 were waited for; matrix products, arithmetic and copies ran while one was open for 2% of the time, Pallas kernels for 20%

profile of v4, /device:TPU:0, one launch (start us, length us, event | category | flops | bytes accessed | tf_op | source)
XLA Modules:
  0.0 242.6 jit_solution(5037127800585939194)
XLA Ops:
  0.0 0.7 compare_convert_fusion
  0.7 0.9 broadcast_multiply_fusion.masked_ref
  1.6 0.0 copy-start
  1.6 2.2 copy-done
  3.8 4.8 %shard_map.64 = (f32[2,16,32,128]{3,2,1,0:T(8,128)S(1)}, f32[2,16,96,128]{3,2,1,0:T(8,128)S(1)}, f32[2,16,32,128]{3,2,1,0:T(8,128)S(1)}, f32[2,16,96,128]{3,2,1,0:T(8,128)}) custom-call(s32[1]{0:T(128)} %bitcast.2.side_ref, bf16[256,8192]{1,0:T(8,128)(2,1)S(1)} %copy-done, bf16[256,128]{1,0:T(8,128)(2,1)S(1)} %broadcast_multiply_fusion.masked_ref), custom_call_target="tpu_custom_call" | custom-call | flops 536870912 | bytes 8388608 | tf_op jit(solution)/shard_map/pallas_call | solution.py:60
  8.6 0.5 collective-permute-start
  9.1 0.1 collective-permute-start.1
  9.1 3.6 %collective-permute-done.1 = f32[2,16,32,128]{3,2,1,0:T(8,128)S(1)} collective-permute-done((f32[2,16,32,128]{3,2,1,0:T(8,128)S(1)}, f32[2,16,32,128]{3,2,1,0:T(8,128)S(1)}, u32[]{:S(2)}, u32[]{:S(2)}) %collective-permute-start.1) | collective-permute-done | bytes 524320 | tf_op jit(solution)/shard_map/ppermute | solution.py:262
  12.8 0.9 add.24
  13.7 6.9 %all-to-all-start.1 = ((f32[32,32,128]{2,1,0:T(8,128)}), f32[32,32,128]{2,1,0:T(8,128)S(1)}, u32[]{:S(2)}, u32[]{:S(2)}) async-start(f32[32,32,128]{2,1,0:T(8,128)} %bitcast.7), calls=%async_computation.1 | async-start | bytes 1048576 | tf_op jit(solution)/shard_map/all_to_all | solution.py:264
  20.6 0.0 collective-permute-done
  20.6 2.8 %add.22 = f32[2,16,96,128]{3,2,1,0:T(8,128)} add(f32[2,16,96,128]{3,2,1,0:T(8,128)S(1)} %get-tuple-element.9, f32[2,16,96,128]{3,2,1,0:T(8,128)} %collective-permute-done) | non-fusion elementwise | flops 393216 | bytes 4718592 | tf_op jit(solution)/shard_map/add | solution.py:263
  23.4 13.1 %all-to-all-done.1 = f32[32,32,128]{2,1,0:T(8,128)S(1)} async-done(((f32[32,32,128]{2,1,0:T(8,128)}), f32[32,32,128]{2,1,0:T(8,128)S(1)}, u32[]{:S(2)}, u32[]{:S(2)}) %all-to-all-start.1) | async-done | bytes 524320 | tf_op jit(solution)/shard_map/all_to_all | solution.py:264
  36.5 0.0 copy-start.1
  36.5 0.0 copy-start.2
  36.5 0.0 copy-start.3
  36.5 2.8 %all-to-all-start = ((f32[32,96,128]{2,1,0:T(8,128)}), f32[32,96,128]{2,1,0:T(8,128)S(1)}, u32[]{:S(2)}, u32[]{:S(2)}) async-start(f32[32,96,128]{2,1,0:T(8,128)} %bitcast.15), calls=%async_computation | async-start | bytes 3145728 | tf_op jit(solution)/shard_map/all_to_all | solution.py:264
  39.4 0.1 pad_add_fusion.place_ref
  39.5 0.1 pad_add_fusion.1.place_ref
  39.5 0.0 copy-done.1
  39.6 0.0 copy-done.2
  39.6 0.0 copy-done.3
  39.6 48.1 %shard_map.65.before_ref = f32[16,4096]{1,0:T(8,128)S(1)} custom-call(s32[2]{0:T(128)S(1)} %pad_add_fusion.1.place_ref, s32[8]{0:T(128)S(1)} %copy-done.3, f32[1024,128]{1,0:T(8,128)S(1)} %bitcast.13, f32[512,128]{1,0:T(8,128)S(1)} %copy-done.1, f32[512,128]{1,0:T(8,128)S(1)} %copy-done.2, f32[16,4096]{1,0:T(8,128)S(1)} %broadcast_in_dim.4.before_ref), custom_call_target="tpu_custom_call" | custom-call | flops 13421772800 | bytes 524288 | tf_op jit(solution)/shard_map/pallas_call | solution.py:151
  87.7 0.0 all-to-all-done
  87.7 142.2 %shard_map.66 = f32[16,4096]{1,0:T(8,128)S(1)} custom-call(s32[2]{0:T(128)S(1)} %pad_add_fusion.place_ref, s32[8]{0:T(128)S(1)} %copy-done.3, f32[3072,128]{1,0:T(8,128)S(1)} %bitcast.12, f32[512,128]{1,0:T(8,128)S(1)} %copy-done.1, f32[512,128]{1,0:T(8,128)S(1)} %copy-done.2, f32[16,4096]{1,0:T(8,128)S(1)} %shard_map.65.before_ref), custom_call_target="tpu_custom_call" | custom-call | flops 40265318400 | bytes 1572864 | tf_op jit(solution)/shard_map/pallas_call | solution.py:151
  230.0 12.0 %shard_map.67 = f32[8,256]{1,0:T(8,128)S(1)} custom-call(f32[32,8,256]{2,1,0:T(8,128)S(1)} %reshape.27.shares_ref), custom_call_target="tpu_custom_call" | custom-call | flops 65536 | bytes 524288 | tf_op jit(solution)/shard_map/pallas_call | solution.py:213
  242.0 0.6 copy.7
  (2 shorter events, 0.1 us)
Async XLA Ops:
  1.6 2.2 copy-start
  8.6 12.0 %collective-permute-start = (f32[2,16,96,128]{3,2,1,0:T(8,128)}, f32[2,16,96,128]{3,2,1,0:T(8,128)}, u32[]{:S(2)}, u32[]{:S(2)}) collective-permute-start(f32[2,16,96,128]{3,2,1,0:T(8,128)} %get-tuple-element.10), channel_id=1, source_target_pairs={{0,1},{1,0},{2,3},{3,2},{4,5},{5,4},{6,7},{7,6},{8,9},{9,8},{10,11... | collective-permute-start | bytes 4718600 | tf_op jit(solution)/shard_map/ppermute | solution.py:262
  9.1 3.7 %collective-permute-start.1 = (f32[2,16,32,128]{3,2,1,0:T(8,128)S(1)}, f32[2,16,32,128]{3,2,1,0:T(8,128)S(1)}, u32[]{:S(2)}, u32[]{:S(2)}) collective-permute-start(f32[2,16,32,128]{3,2,1,0:T(8,128)S(1)} %get-tuple-element.12), channel_id=1, source_target_pairs={{0,1},{1,0},{2,3},{3,2},{4,5},{5,4},{6,7},{7,6},{8,9},{9,8},{10,11... | collective-permute-start | bytes 1572872 | tf_op jit(solution)/shard_map/ppermute | solution.py:262
  13.7 22.9 %all-to-all-start.1 = ((f32[32,32,128]{2,1,0:T(8,128)}), f32[32,32,128]{2,1,0:T(8,128)S(1)}, u32[]{:S(2)}, u32[]{:S(2)}) async-start(f32[32,32,128]{2,1,0:T(8,128)} %bitcast.7), calls=%async_computation.1 | async-start | bytes 1048576 | tf_op jit(solution)/shard_map/all_to_all | solution.py:264
  36.5 3.0 %copy-start.1 = (f32[512,128]{1,0:T(8,128)S(1)}, f32[512,128]{1,0:T(8,128)}, u32[]{:S(2)}) copy-start(f32[512,128]{1,0:T(8,128)} %one_ref.3) | copy-start | bytes 786436
  36.5 3.0 %copy-start.2 = (f32[512,128]{1,0:T(8,128)S(1)}, f32[512,128]{1,0:T(8,128)}, u32[]{:S(2)}) copy-start(f32[512,128]{1,0:T(8,128)} %two_ref.3) | copy-start | bytes 786436
  36.5 3.0 %copy-start.3 = (s32[8]{0:T(128)S(1)}, s32[8]{0:T(128)}, u32[]{:S(2)}) copy-start(s32[8]{0:T(128)} %seeds_ref.3) | copy-start | bytes 100
  36.5 51.2 %all-to-all-start = ((f32[32,96,128]{2,1,0:T(8,128)}), f32[32,96,128]{2,1,0:T(8,128)S(1)}, u32[]{:S(2)}, u32[]{:S(2)}) async-start(f32[32,96,128]{2,1,0:T(8,128)} %bitcast.15), calls=%async_computation | async-start | bytes 3145728 | tf_op jit(solution)/shard_map/all_to_all | solution.py:264

commit v5 on v4

--- a/solution.py
+++ b/solution.py
@@ -20,7 +20,8 @@
 
 GRAD_COLUMNS = 1024
 TILE_ROWS = 2
-BODY_ROWS = 16
+BODY_ROWS = 32
+AHEAD_BODY = 24
 STRIP = 32
 PASS_COLUMNS = 256
 
@@ -86,11 +87,70 @@
     return jnp.where(hashed < 0, -1.0, 1.0).astype(jnp.bfloat16)
 
 
+def fill_base(block_number, seeds_ref, base):
+    column = lax.broadcasted_iota(jnp.int32, base.shape, 0)
+    feature = block_number * FEAT_BLOCK + lax.broadcasted_iota(jnp.int32, base.shape, 1)
+    base[...] = seeds_ref[block_number] + feature * mix_feature + column * mix_param
+
+
+def row_offset(row, piece, half, rank, place_ref):
+    side = row // piece
+    return (place_ref[1] + side * half + (row - side * piece)) * jnp.int32(wrapped(mix_param * rank))
+
+
+def sign_tile(base, row, columns, piece, half, place_ref):
+    rank = base.shape[0]
+    return jnp.concatenate(
+        [
+            sign_strip(
+                base[strip : strip + STRIP, columns] + row_offset(row + step, piece, half, rank, place_ref)
+            )
+            for step in range(TILE_ROWS)
+            for strip in range(0, rank, STRIP)
+        ],
+        axis=0,
+    )
+
+
+def column_parts():
+    return [slice(start, start + PASS_COLUMNS) for start in range(0, FEAT_BLOCK, PASS_COLUMNS)]
+
+
+def ahead_kernel(shape, place_ref, seeds_ref, out_ref, base):
+    piece, half, body_rows = shape
+    fill_base(pl.program_id(0), seeds_ref, base)
+    depth = TILE_ROWS * base.shape[0]
+    for index in range(2 * piece // body_rows):
+        row = (index + 1) * body_rows - TILE_ROWS
+        for columns in column_parts():
+            out_ref[index * depth : (index + 1) * depth, columns] = sign_tile(
+                base, row, columns, piece, half, place_ref
+            )
+
+
+def hash_ahead(place, seeds, piece, half, rank, body_rows):
+    features = seeds.shape[0] * FEAT_BLOCK
+    depth = 2 * piece // body_rows * TILE_ROWS * rank
+    return pl.pallas_call(
+        functools.partial(ahead_kernel, (piece, half, body_rows)),
+        grid=(seeds.shape[0],),
+        in_specs=[pl.BlockSpec(memory_space=pltpu.SMEM)] * 2,
+        out_specs=pl.BlockSpec((depth, FEAT_BLOCK), lambda block: (0, block)),
+        out_shape=jax.ShapeDtypeStruct((depth, features), jnp.bfloat16),
+        scratch_shapes=[pltpu.VMEM((rank, FEAT_BLOCK), jnp.int32)],
+        compiler_params=pltpu.CompilerParams(vmem_limit_bytes=32 * 2**20),
+        cost_estimate=pl.CostEstimate(
+            flops=1600 * depth * features, bytes_accessed=2 * depth * features, transcendentals=0
+        ),
+    )(place, seeds)
+
+
 def project_kernel(
-    shape, place_ref, seeds_ref, grad_ref, one_ref, two_ref, before_ref, out_ref,
-    directions, base,
+    shape, place_ref, seeds_ref, grad_ref, one_ref, two_ref, before_ref, *refs,
 ):
-    sequences, piece, half, rank, scale = shape
+    ahead_ref = refs[0] if len(refs) == 4 else None
+    out_ref, directions, base = refs[-3:]
+    sequences, piece, half, rank, scale, body_rows = shape
     block_number = pl.program_id(0)
     rows = 2 * piece
 
@@ -108,48 +168,41 @@
 
             lax.fori_loop(0, piece, prepare, 0)
 
-    column = lax.broadcasted_iota(jnp.int32, base.shape, 0)
-    feature = block_number * FEAT_BLOCK + lax.broadcasted_iota(jnp.int32, base.shape, 1)
-    base[...] = seeds_ref[block_number] + feature * mix_feature + column * mix_param
-    row_step = jnp.int32(wrapped(mix_param * rank))
-
-    passes = FEAT_BLOCK // PASS_COLUMNS
+    fill_base(block_number, seeds_ref, base)
+    depth = TILE_ROWS * rank
+    parts = column_parts()
 
     def body(index, sums):
         sums = list(sums)
-        for tile in range(BODY_ROWS // TILE_ROWS):
-            row = index * BODY_ROWS + tile * TILE_ROWS
-            side = row // piece
-            first = place_ref[1] + side * half + (row - side * piece)
+        for tile in range(body_rows // TILE_ROWS):
+            row = index * body_rows + tile * TILE_ROWS
             directed = jnp.concatenate(
                 [directions[row + step] for step in range(TILE_ROWS)], axis=1
             )
-            for part in range(passes):
-                columns = slice(part * PASS_COLUMNS, (part + 1) * PASS_COLUMNS)
-                signs = jnp.concatenate(
-                    [
-                        sign_strip(base[strip : strip + STRIP, columns] + (first + step) * row_step)
-                        for step in range(TILE_ROWS)
-                        for strip in range(0, rank, STRIP)
-                    ],
-                    axis=0,
-                )
+            ready = ahead_ref is not None and tile == body_rows // TILE_ROWS - 1
+            for part, columns in enumerate(parts):
+                if ready:
+                    signs = ahead_ref[pl.ds(pl.multiple_of(index * depth, depth), depth), columns]
+                else:
+                    signs = sign_tile(base, row, columns, piece, half, place_ref)
                 sums[part] += jnp.dot(directed, signs, preferred_element_type=jnp.float32)
         return tuple(sums)
 
     zero = jnp.zeros((sequences, PASS_COLUMNS), jnp.float32)
-    sums = lax.fori_loop(0, rows // BODY_ROWS, body, (zero,) * passes)
+    sums = lax.fori_loop(0, rows // body_rows, body, (zero,) * len(parts))
     out_ref[...] = before_ref[...] + jnp.concatenate(sums, axis=1) * scale
 
 
-def project(place, seeds, received, moment_one, moment_two, before, sequences, piece, half, scale):
+def project(
+    place, seeds, received, moment_one, moment_two, before, ahead, sequences, piece, half, scale, body_rows
+):
     rank = received.shape[1]
     features = seeds.shape[0] * FEAT_BLOCK
     rows = 2 * piece
     whole = lambda array: pl.BlockSpec(array.shape, lambda block: (0, 0))
     part = pl.BlockSpec((sequences, FEAT_BLOCK), lambda block: (0, block))
     return pl.pallas_call(
-        functools.partial(project_kernel, (sequences, piece, half, rank, scale)),
+        functools.partial(project_kernel, (sequences, piece, half, rank, scale, body_rows)),
         grid=(seeds.shape[0],),
         in_specs=[
             pl.BlockSpec(memory_space=pltpu.SMEM),
@@ -158,7 +211,8 @@
             whole(moment_one),
             whole(moment_two),
             part,
-        ],
+        ]
+        + [pl.BlockSpec((array.shape[0], FEAT_BLOCK), lambda block: (0, block)) for array in ahead],
         out_specs=part,
         out_shape=jax.ShapeDtypeStruct((sequences, features), jnp.float32),
         scratch_shapes=[
@@ -169,7 +223,7 @@
         cost_estimate=pl.CostEstimate(
             flops=400 * rows * rank * features, bytes_accessed=4 * received.size, transcendentals=0
         ),
-    )(place, seeds, received, moment_one, moment_two, before)
+    )(place, seeds, received, moment_one, moment_two, before, *ahead)
 
 
 def gather_kernel(groups, device_list, shares_ref, out_ref, landing, send_sem, recv_sem):
@@ -257,20 +311,30 @@
     blocks = half_gradients(hidden_input_rows, masked_values, side, device_list, groups, half, pieces)
     chunks = len(pieces)
     pairs = [(source, source ^ 1) for source in range(device_list)]
+    places = []
+    for offset, _ in pieces:
+        in_slice = my_group * owned + offset
+        places.append(jnp.stack([in_slice, my_index * local_rows + in_slice]).astype(jnp.int32))
+    partials = jnp.zeros((sequences, block_seeds.shape[0] * FEAT_BLOCK), jnp.float32)
+    late_rows = 2 * pieces[1][1]
+    late_body = AHEAD_BODY if late_rows % AHEAD_BODY == 0 else math.gcd(late_rows, BODY_ROWS)
     received = []
+    ahead = []
     for chunk, (_, piece) in enumerate(pieces):
         other = lax.ppermute(blocks[chunks + chunk], "dp", pairs)
         summed = (blocks[chunk] + other).reshape(devices, piece, rank)
+        if chunk == 0:
+            late_place, summed = lax.optimization_barrier((places[1], summed))
+            ahead = [hash_ahead(late_place, block_seeds, pieces[1][1], half, rank, late_body)]
+            partials, *ahead = lax.optimization_barrier((partials, *ahead))
         gathered = lax.all_to_all(summed, axes, split_axis=0, concat_axis=0, tiled=True)
         received.append(gathered.reshape(devices * piece, rank))
 
-    partials = jnp.zeros((sequences, block_seeds.shape[0] * FEAT_BLOCK), jnp.float32)
-    for chunk, (offset, piece) in enumerate(pieces):
-        in_slice = my_group * owned + offset
-        place = jnp.stack([in_slice, my_index * local_rows + in_slice]).astype(jnp.int32)
+    for chunk, (_, piece) in enumerate(pieces):
+        body_rows = late_body if chunk else math.gcd(2 * piece, BODY_ROWS)
         partials = project(
-            place, block_seeds, received[chunk], adam_first_moment, adam_second_moment, partials,
-            sequences, piece, half, scale,
+            places[chunk], block_seeds, received[chunk], adam_first_moment, adam_second_moment, partials,
+            ahead if chunk else [], sequences, piece, half, scale, body_rows,
         )
     shares = partials.reshape(devices, 8, -1)
     return sum_shares(shares, groups, device_list).reshape(1, -1)

time: 243 us -> 254 us (1.045)
  local copies, waits for them, and re-layouts: 2.87 us -> 14.4 us
    pallas_call x2, Pallas kernels: 190 us -> 177 us  [project(): pl.pallas_call(functools.partial(project_kernel, (sequences, piece, half,...]
    pallas_call x0 -> x1, Pallas kernels: none -> 12.4 us  [hash_ahead(): pl.pallas_call(functools.partial(ahead_kernel, (piece, half, body_rows)),...]
    unnamed x9 -> x13, local copies, waits for them, and re-layouts: 2.8 us -> 14.3 us
  transfers between devices with their start and end apart: 4 -> 4, of which waited for: 2 -> 2; matrix products, arithmetic and copies ran while one was open for 2% -> 2% of each run, Pallas kernels for 20% -> 23%
where the time goes in v5:
time: 254 us
  Pallas kernels  207 us (81%)
  waiting for transfers between devices  16.7 us (7%)
  local copies, waits for them, and re-layouts  14.4 us (6%)
  starting transfers between devices  10.3 us (4%)
  other arithmetic  5.44 us (2%)
    pallas_call x2, Pallas kernels, project(): pl.pallas_call(functools.partial(project_kernel, (sequences, piece, half,...  177 us
    unnamed x13, local copies, waits for them, and re-layouts  14.3 us
    all_to_all x2, waiting for transfers between devices, local(): lax.all_to_all(summed, axes, split_axis=0, concat_axis=0, tiled=True)  13.1 us
    pallas_call x1, Pallas kernels, hash_ahead(): pl.pallas_call(functools.partial(ahead_kernel, (piece, half, body_rows)),...  12.4 us
    pallas_call x1, Pallas kernels, sum_shares(): pl.pallas_call(functools.partial(gather_kernel, groups, device_list), in_...  12 us
    all_to_all x2, starting transfers between devices, local(): lax.all_to_all(summed, axes, split_axis=0, concat_axis=0, tiled=True)  9.75 us
  transfers between devices with their start and end apart: 4, of which 2 were waited for; matrix products, arithmetic and copies ran while one was open for 2% of the time, Pallas kernels for 23%

profile of v5, /device:TPU:0, one launch (start us, length us, event | category | flops | bytes accessed | tf_op | source)
XLA Modules:
  0.0 253.5 jit_solution(17000721384933073549)
XLA Ops:
  0.0 0.7 compare_convert_fusion
  0.7 0.9 broadcast_multiply_fusion.masked_ref
  1.6 0.0 copy-start
  1.6 2.2 copy-done
  3.8 4.8 %shard_map.64 = (f32[2,16,32,128]{3,2,1,0:T(8,128)S(1)}, f32[2,16,96,128]{3,2,1,0:T(8,128)S(1)}, f32[2,16,32,128]{3,2,1,0:T(8,128)S(1)}, f32[2,16,96,128]{3,2,1,0:T(8,128)}) custom-call(s32[1]{0:T(128)} %bitcast.2.side_ref, bf16[256,8192]{1,0:T(8,128)(2,1)S(1)} %copy-done, bf16[256,128]{1,0:T(8,128)(2,1)S(1)} %broadcast_multiply_fusion.masked_ref), custom_call_target="tpu_custom_call" | custom-call | flops 536870912 | bytes 8388608 | tf_op jit(solution)/shard_map/pallas_call | solution.py:61
  8.6 0.4 collective-permute-start
  9.1 0.1 collective-permute-start.1
  9.2 0.1 pad_add_fusion.place_ref
  9.2 3.6 %collective-permute-done.1 = f32[2,16,32,128]{3,2,1,0:T(8,128)S(1)} collective-permute-done((f32[2,16,32,128]{3,2,1,0:T(8,128)S(1)}, f32[2,16,32,128]{3,2,1,0:T(8,128)S(1)}, u32[]{:S(2)}, u32[]{:S(2)}) %collective-permute-start.1) | collective-permute-done | bytes 524320 | tf_op jit(solution)/shard_map/ppermute | solution.py:324
  12.8 0.9 add.24
  13.7 6.9 %all-to-all-start.1 = ((f32[32,32,128]{2,1,0:T(8,128)}), f32[32,32,128]{2,1,0:T(8,128)S(1)}, u32[]{:S(2)}, u32[]{:S(2)}) async-start(f32[32,32,128]{2,1,0:T(8,128)} %bitcast.7), calls=%async_computation.1 | async-start | bytes 1048576 | tf_op jit(solution)/shard_map/all_to_all | solution.py:330
  20.6 0.0 collective-permute-done
  20.6 2.8 %add.22 = f32[2,16,96,128]{3,2,1,0:T(8,128)} add(f32[2,16,96,128]{3,2,1,0:T(8,128)S(1)} %get-tuple-element.13, f32[2,16,96,128]{3,2,1,0:T(8,128)} %collective-permute-done) | non-fusion elementwise | flops 393216 | bytes 4718592 | tf_op jit(solution)/shard_map/add | solution.py:325
  23.4 13.1 %all-to-all-done.1 = f32[32,32,128]{2,1,0:T(8,128)S(1)} async-done(((f32[32,32,128]{2,1,0:T(8,128)}), f32[32,32,128]{2,1,0:T(8,128)S(1)}, u32[]{:S(2)}, u32[]{:S(2)}) %all-to-all-start.1) | async-done | bytes 524320 | tf_op jit(solution)/shard_map/all_to_all | solution.py:330
  36.5 0.0 copy-start.3
  36.5 2.8 %all-to-all-start = ((f32[32,96,128]{2,1,0:T(8,128)}), f32[32,96,128]{2,1,0:T(8,128)S(1)}, u32[]{:S(2)}, u32[]{:S(2)}) async-start(f32[32,96,128]{2,1,0:T(8,128)} %bitcast.15), calls=%async_computation | async-start | bytes 3145728 | tf_op jit(solution)/shard_map/all_to_all | solution.py:330
  39.4 0.1 pad_add_fusion.1.place_ref
  39.4 0.0 copy-done.3
  39.5 0.0 copy-start.1
  39.5 0.0 copy-start.2
  39.5 12.4 %shard_map.65.refs_0_ = bf16[2048,4096]{1,0:T(8,128)(2,1)S(1)} custom-call(s32[2]{0:T(128)S(1)} %pad_add_fusion.place_ref, s32[8]{0:T(128)S(1)} %copy-done.3), custom_call_target="tpu_custom_call" | custom-call | flops 13421772800 | bytes 16777216 | tf_op jit(solution)/shard_map/pallas_call | solution.py:134
  51.9 0.0 copy-start.4
  51.9 5.7 %copy-done.4 = bf16[2048,4096]{1,0:T(8,128)(2,1)} copy-done((bf16[2048,4096]{1,0:T(8,128)(2,1)}, bf16[2048,4096]{1,0:T(8,128)(2,1)S(1)}, u32[]{:S(2)}) %copy-start.4) | copy-done | bytes 16777240
  57.6 0.0 copy-done.1
  57.6 0.0 copy-done.2
  57.6 46.1 %shard_map.66.before_ref = f32[16,4096]{1,0:T(8,128)S(1)} custom-call(s32[2]{0:T(128)S(1)} %pad_add_fusion.1.place_ref, s32[8]{0:T(128)S(1)} %copy-done.3, f32[1024,128]{1,0:T(8,128)S(1)} %bitcast.13, f32[512,128]{1,0:T(8,128)S(1)} %copy-done.1, f32[512,128]{1,0:T(8,128)S(1)} %copy-done.2, f32[16,4096]{1,0:T(8,128)S(1)} %broadcast_in_dim.4.before_ref), custom_call_target="tpu_custom_call" | custom-call | flops 13421772800 | bytes 524288 | tf_op jit(solution)/shard_map/pallas_call | solution.py:204
  103.8 0.0 all-to-all-done
  103.8 0.0 copy-start.5
  103.8 5.8 %copy-done.5 = bf16[2048,4096]{1,0:T(8,128)(2,1)S(1)} copy-done((bf16[2048,4096]{1,0:T(8,128)(2,1)S(1)}, bf16[2048,4096]{1,0:T(8,128)(2,1)}, u32[]{:S(2)}) %copy-start.5) | copy-done | bytes 16777240
  109.6 131.3 %shard_map.67 = f32[16,4096]{1,0:T(8,128)S(1)} custom-call(s32[2]{0:T(128)S(1)} %pad_add_fusion.place_ref, s32[8]{0:T(128)S(1)} %copy-done.3, f32[3072,128]{1,0:T(8,128)S(1)} %bitcast.12, f32[512,128]{1,0:T(8,128)S(1)} %copy-done.1, f32[512,128]{1,0:T(8,128)S(1)} %copy-done.2, f32[16,4096]{1,0:T(8,128)S(1)} %shard_map.66.before_ref, ...), custom_call_target="tpu_custom_call" | custom-call | flops 40265318400 | bytes 1572864 | tf_op jit(solution)/shard_map/pallas_call | solution.py:204
  240.9 12.0 %shard_map.68 = f32[8,256]{1,0:T(8,128)S(1)} custom-call(f32[32,8,256]{2,1,0:T(8,128)S(1)} %reshape.27.shares_ref), custom_call_target="tpu_custom_call" | custom-call | flops 65536 | bytes 524288 | tf_op jit(solution)/shard_map/pallas_call | solution.py:267
  252.9 0.6 copy.7
  (2 shorter events, 0.1 us)
Async XLA Ops:
  1.6 2.2 copy-start
  8.6 12.0 %collective-permute-start = (f32[2,16,96,128]{3,2,1,0:T(8,128)}, f32[2,16,96,128]{3,2,1,0:T(8,128)}, u32[]{:S(2)}, u32[]{:S(2)}) collective-permute-start(f32[2,16,96,128]{3,2,1,0:T(8,128)} %get-tuple-element.14), channel_id=1, source_target_pairs={{0,1},{1,0},{2,3},{3,2},{4,5},{5,4},{6,7},{7,6},{8,9},{9,8},{10,11... | collective-permute-start | bytes 4718600 | tf_op jit(solution)/shard_map/ppermute | solution.py:324
  9.1 3.7 %collective-permute-start.1 = (f32[2,16,32,128]{3,2,1,0:T(8,128)S(1)}, f32[2,16,32,128]{3,2,1,0:T(8,128)S(1)}, u32[]{:S(2)}, u32[]{:S(2)}) collective-permute-start(f32[2,16,32,128]{3,2,1,0:T(8,128)S(1)} %get-tuple-element.16), channel_id=1, source_target_pairs={{0,1},{1,0},{2,3},{3,2},{4,5},{5,4},{6,7},{7,6},{8,9},{9,8},{10,11... | collective-permute-start | bytes 1572872 | tf_op jit(solution)/shard_map/ppermute | solution.py:324
  13.7 22.8 %all-to-all-start.1 = ((f32[32,32,128]{2,1,0:T(8,128)}), f32[32,32,128]{2,1,0:T(8,128)S(1)}, u32[]{:S(2)}, u32[]{:S(2)}) async-start(f32[32,32,128]{2,1,0:T(8,128)} %bitcast.7), calls=%async_computation.1 | async-start | bytes 1048576 | tf_op jit(solution)/shard_map/all_to_all | solution.py:330
  36.5 2.9 %copy-start.3 = (s32[8]{0:T(128)S(1)}, s32[8]{0:T(128)}, u32[]{:S(2)}) copy-start(s32[8]{0:T(128)} %seeds_ref.5) | copy-start | bytes 100
  36.5 67.2 %all-to-all-start = ((f32[32,96,128]{2,1,0:T(8,128)}), f32[32,96,128]{2,1,0:T(8,128)S(1)}, u32[]{:S(2)}, u32[]{:S(2)}) async-start(f32[32,96,128]{2,1,0:T(8,128)} %bitcast.15), calls=%async_computation | async-start | bytes 3145728 | tf_op jit(solution)/shard_map/all_to_all | solution.py:330
  39.5 18.2 %copy-start.1 = (f32[512,128]{1,0:T(8,128)S(1)}, f32[512,128]{1,0:T(8,128)}, u32[]{:S(2)}) copy-start(f32[512,128]{1,0:T(8,128)} %one_ref.3) | copy-start | bytes 786436
  39.5 18.2 %copy-start.2 = (f32[512,128]{1,0:T(8,128)S(1)}, f32[512,128]{1,0:T(8,128)}, u32[]{:S(2)}) copy-start(f32[512,128]{1,0:T(8,128)} %two_ref.3) | copy-start | bytes 786436
  51.9 5.7 %copy-start.4 = (bf16[2048,4096]{1,0:T(8,128)(2,1)}, bf16[2048,4096]{1,0:T(8,128)(2,1)S(1)}, u32[]{:S(2)}) copy-start(bf16[2048,4096]{1,0:T(8,128)(2,1)S(1)} %shard_map.65.refs_0_) | copy-start | bytes 50331652
  103.8 5.8 %copy-start.5 = (bf16[2048,4096]{1,0:T(8,128)(2,1)S(1)}, bf16[2048,4096]{1,0:T(8,128)(2,1)}, u32[]{:S(2)}) copy-start(bf16[2048,4096]{1,0:T(8,128)(2,1)} %copy-done.4) | copy-start | bytes 50331652

commit v6 on v5

--- a/solution.py
+++ b/solution.py
@@ -84,7 +84,7 @@
     hashed = hashed * mix_round
     hashed = hashed ^ lax.shift_right_logical(hashed, jnp.full_like(hashed, 16))
     hashed = hashed * mix_round
-    return jnp.where(hashed < 0, -1.0, 1.0).astype(jnp.bfloat16)
+    return jnp.where(hashed < 0, jnp.bfloat16(-1), jnp.bfloat16(1))
 
 
 def fill_base(block_number, seeds_ref, base):
@@ -138,7 +138,7 @@
         out_specs=pl.BlockSpec((depth, FEAT_BLOCK), lambda block: (0, block)),
         out_shape=jax.ShapeDtypeStruct((depth, features), jnp.bfloat16),
         scratch_shapes=[pltpu.VMEM((rank, FEAT_BLOCK), jnp.int32)],
-        compiler_params=pltpu.CompilerParams(vmem_limit_bytes=32 * 2**20),
+        compiler_params=pltpu.CompilerParams(vmem_limit_bytes=56 * 2**20),
         cost_estimate=pl.CostEstimate(
             flops=1600 * depth * features, bytes_accessed=2 * depth * features, transcendentals=0
         ),
@@ -219,7 +219,7 @@
             pltpu.VMEM((rows, sequences, rank), jnp.bfloat16),
             pltpu.VMEM((rank, FEAT_BLOCK), jnp.int32),
         ],
-        compiler_params=pltpu.CompilerParams(vmem_limit_bytes=32 * 2**20),
+        compiler_params=pltpu.CompilerParams(vmem_limit_bytes=56 * 2**20),
         cost_estimate=pl.CostEstimate(
             flops=400 * rows * rank * features, bytes_accessed=4 * received.size, transcendentals=0
         ),
@@ -326,7 +326,8 @@
         if chunk == 0:
             late_place, summed = lax.optimization_barrier((places[1], summed))
             ahead = [hash_ahead(late_place, block_seeds, pieces[1][1], half, rank, late_body)]
-            partials, *ahead = lax.optimization_barrier((partials, *ahead))
+        else:
+            summed, *ahead = lax.optimization_barrier((summed, *ahead))
         gathered = lax.all_to_all(summed, axes, split_axis=0, concat_axis=0, tiled=True)
         received.append(gathered.reshape(devices * piece, rank))
 

time: 254 us -> 222 us (0.87)
  waiting for transfers between devices: 16.7 us -> 1.58 us
  Pallas kernels: 207 us -> 193 us
  local copies, waits for them, and re-layouts: 14.4 us -> 6.43 us
  starting transfers between devices: 10.3 us -> 13.6 us
    pallas_call x2, Pallas kernels: 177 us -> 164 us  [project(): pl.pallas_call(functools.partial(project_kernel, (sequences, piece, half,...]
    all_to_all x2, waiting for transfers between devices: 13.1 us -> 0.54 us  [local(): lax.all_to_all(summed, axes, split_axis=0, concat_axis=0, tiled=True)]
    unnamed x13 -> x7, local copies, waits for them, and re-layouts: 14.3 us -> 4.72 us
    all_to_all x2, starting transfers between devices: 9.75 us -> 13.1 us  [local(): lax.all_to_all(summed, axes, split_axis=0, concat_axis=0, tiled=True)]
  transfers between devices with their start and end apart: 4 -> 4, of which waited for: 2 -> 2; matrix products, arithmetic and copies ran while one was open for 2% -> 2% of each run, Pallas kernels for 23% -> 25%
where the time goes in v6:
time: 222 us; the launch traced here: 221 us
  Pallas kernels  193 us (87%)
  starting transfers between devices  13.6 us (6%)
  other arithmetic  6.43 us (3%)
  local copies, waits for them, and re-layouts  6.43 us (3%)
    pallas_call x2, Pallas kernels, project(): pl.pallas_call(functools.partial(project_kernel, (sequences, piece, half,...  164 us
    all_to_all x2, starting transfers between devices, local(): lax.all_to_all(summed, axes, split_axis=0, concat_axis=0, tiled=True)  13.1 us
    pallas_call x1, Pallas kernels, hash_ahead(): pl.pallas_call(functools.partial(ahead_kernel, (piece, half, body_rows)),...  12.6 us
    pallas_call x1, Pallas kernels, sum_shares(): pl.pallas_call(functools.partial(gather_kernel, groups, device_list), in_...  12.1 us
    pallas_call x1, Pallas kernels, half_gradients(): pl.pallas_call(functools.partial(grad_kernel, (local_rows, groups, half,...  4.78 us
    unnamed x7, local copies, waits for them, and re-layouts  4.72 us
  transfers between devices with their start and end apart: 4, of which 2 were waited for; matrix products, arithmetic and copies ran while one was open for 2% of the time, Pallas kernels for 25%

profile of v6, /device:TPU:0, one launch (start us, length us, event | category | flops | bytes accessed | tf_op | source)
XLA Modules:
  0.0 221.2 jit_solution(17285709082220114908)
XLA Ops:
  0.0 0.7 compare_convert_fusion
  0.7 0.9 broadcast_multiply_fusion.masked_ref
  1.6 0.0 copy-start
  1.6 2.2 copy-done
  3.8 4.8 %shard_map.64 = (f32[2,16,32,128]{3,2,1,0:T(8,128)S(1)}, f32[2,16,96,128]{3,2,1,0:T(8,128)S(1)}, f32[2,16,32,128]{3,2,1,0:T(8,128)S(1)}, f32[2,16,96,128]{3,2,1,0:T(8,128)}) custom-call(s32[1]{0:T(128)} %bitcast.2.side_ref, bf16[256,8192]{1,0:T(8,128)(2,1)S(1)} %copy-done, bf16[256,128]{1,0:T(8,128)(2,1)S(1)} %broadcast_multiply_fusion.masked_ref), custom_call_target="tpu_custom_call" | custom-call | flops 536870912 | bytes 8388608 | tf_op jit(solution)/shard_map/pallas_call | solution.py:61
  8.6 0.5 collective-permute-start.1
  9.1 0.1 collective-permute-start
  9.1 0.6 pad_add_fusion.place_ref
  9.7 1.0 collective-permute-done.1
  10.7 0.9 add.23
  11.6 7.8 %all-to-all-start.1 = ((f32[32,32,128]{2,1,0:T(8,128)}), f32[32,32,128]{2,1,0:T(8,128)S(1)}, u32[]{:S(2)}, u32[]{:S(2)}) async-start(f32[32,32,128]{2,1,0:T(8,128)} %bitcast.4), calls=%async_computation.1 | async-start | bytes 1048576 | tf_op jit(solution)/shard_map/all_to_all | solution.py:331
  19.4 12.6 %shard_map.65.refs_0_ = bf16[2048,4096]{1,0:T(8,128)(2,1)} custom-call(s32[2]{0:T(128)} %pad_add_fusion.place_ref, s32[8]{0:T(128)} %seeds_ref.5), custom_call_target="tpu_custom_call" | custom-call | flops 13421772800 | bytes 16777216 | tf_op jit(solution)/shard_map/pallas_call | solution.py:134
  32.0 0.0 collective-permute-done
  32.0 2.8 %add.22 = f32[2,16,96,128]{3,2,1,0:T(8,128)} add(f32[2,16,96,128]{3,2,1,0:T(8,128)S(1)} %get-tuple-element.13, f32[2,16,96,128]{3,2,1,0:T(8,128)} %collective-permute-done) | non-fusion elementwise | flops 393216 | bytes 4718592 | tf_op jit(solution)/shard_map/add | solution.py:325
  34.8 0.5 all-to-all-done.1
  35.3 0.0 copy-start.2
  35.3 0.8 copy-done.2
  36.1 5.3 %all-to-all-start = ((f32[32,96,128]{2,1,0:T(8,128)}), f32[32,96,128]{2,1,0:T(8,128)S(1)}, u32[]{:S(2)}, u32[]{:S(2)}) async-start(f32[32,96,128]{2,1,0:T(8,128)} %bitcast.3), calls=%async_computation | async-start | bytes 3145728 | tf_op jit(solution)/shard_map/all_to_all | solution.py:331
  41.4 0.6 pad_add_fusion.1.place_ref
  42.0 0.7 broadcast_in_dim.4.before_ref
  42.7 43.1 %shard_map.66.before_ref = f32[16,4096]{1,0:T(8,128)} custom-call(s32[2]{0:T(128)} %pad_add_fusion.1.place_ref, s32[8]{0:T(128)} %seeds_ref.5, f32[1024,128]{1,0:T(8,128)} %bitcast.14, f32[512,128]{1,0:T(8,128)} %one_ref.3, f32[512,128]{1,0:T(8,128)} %two_ref.3, f32[16,4096]{1,0:T(8,128)} %broadcast_in_dim.4.before_ref), custom_call_target="tpu_custom_call" | custom-call | flops 13421772800 | bytes 524288 | tf_op jit(solution)/shard_map/pallas_call | solution.py:204
  85.8 0.0 all-to-all-done
  85.8 0.0 copy-start.1
  85.8 1.1 copy-done.1
  86.9 120.6 %shard_map.67 = f32[16,4096]{1,0:T(8,128)} custom-call(s32[2]{0:T(128)} %pad_add_fusion.place_ref, s32[8]{0:T(128)} %seeds_ref.5, f32[3072,128]{1,0:T(8,128)} %bitcast.13, f32[512,128]{1,0:T(8,128)} %one_ref.3, f32[512,128]{1,0:T(8,128)} %two_ref.3, f32[16,4096]{1,0:T(8,128)} %shard_map.66.before_ref, bf16[2048,4096]{1,0:T(8,128)(2,1)} %shard_map.65.refs_0_), custom_call_target="tpu_custom_call" | custom-call | flops 40265318400 | bytes 1572864 | tf_op jit(solution)/shard_map/pallas_call | solution.py:204
  207.5 1.0 reshape.27.shares_ref
  208.5 12.1 %shard_map.68 = f32[8,256]{1,0:T(8,128)S(1)} custom-call(f32[32,8,256]{2,1,0:T(8,128)S(1)} %reshape.27.shares_ref), custom_call_target="tpu_custom_call" | custom-call | flops 65536 | bytes 524288 | tf_op jit(solution)/shard_map/pallas_call | solution.py:267
  220.6 0.6 copy.7
Async XLA Ops:
  1.6 2.2 copy-start
  8.6 2.1 collective-permute-start.1
  9.1 23.0 %collective-permute-start = (f32[2,16,96,128]{3,2,1,0:T(8,128)}, f32[2,16,96,128]{3,2,1,0:T(8,128)}, u32[]{:S(2)}, u32[]{:S(2)}) collective-permute-start(f32[2,16,96,128]{3,2,1,0:T(8,128)} %get-tuple-element.14), channel_id=1, source_target_pairs={{0,1},{1,0},{2,3},{3,2},{4,5},{5,4},{6,7},{7,6},{8,9},{9,8},{10,11... | collective-permute-start | bytes 4718600 | tf_op jit(solution)/shard_map/ppermute | solution.py:324
  11.6 23.7 %all-to-all-start.1 = ((f32[32,32,128]{2,1,0:T(8,128)}), f32[32,32,128]{2,1,0:T(8,128)S(1)}, u32[]{:S(2)}, u32[]{:S(2)}) async-start(f32[32,32,128]{2,1,0:T(8,128)} %bitcast.4), calls=%async_computation.1 | async-start | bytes 1048576 | tf_op jit(solution)/shard_map/all_to_all | solution.py:331
  35.3 0.8 copy-start.2
  36.1 49.7 %all-to-all-start = ((f32[32,96,128]{2,1,0:T(8,128)}), f32[32,96,128]{2,1,0:T(8,128)S(1)}, u32[]{:S(2)}, u32[]{:S(2)}) async-start(f32[32,96,128]{2,1,0:T(8,128)} %bitcast.3), calls=%async_computation | async-start | bytes 3145728 | tf_op jit(solution)/shard_map/all_to_all | solution.py:331
  85.8 1.2 copy-start.1

commit v7 on v6

--- a/solution.py
+++ b/solution.py
@@ -20,8 +20,8 @@
 
 GRAD_COLUMNS = 1024
 TILE_ROWS = 2
-BODY_ROWS = 32
-AHEAD_BODY = 24
+BODY_ROWS = 64
+AHEAD_STRIDE = 24
 STRIP = 32
 PASS_COLUMNS = 256
 
@@ -72,7 +72,7 @@
         out_shape=[
             jax.ShapeDtypeStruct((groups, device_list, size, rank), jnp.float32) for size in sizes
         ],
-        compiler_params=pltpu.CompilerParams(vmem_limit_bytes=32 * 2**20),
+        compiler_params=pltpu.CompilerParams(vmem_limit_bytes=60 * 2**20),
         cost_estimate=pl.CostEstimate(
             flops=2 * tokens * width * rank, bytes_accessed=2 * tokens * width + 4 * width * rank, transcendentals=0
         ),
@@ -150,7 +150,7 @@
 ):
     ahead_ref = refs[0] if len(refs) == 4 else None
     out_ref, directions, base = refs[-3:]
-    sequences, piece, half, rank, scale, body_rows = shape
+    sequences, piece, half, rank, scale, body_rows, stride = shape
     block_number = pl.program_id(0)
     rows = 2 * piece
 
@@ -179,10 +179,11 @@
             directed = jnp.concatenate(
                 [directions[row + step] for step in range(TILE_ROWS)], axis=1
             )
-            ready = ahead_ref is not None and tile == body_rows // TILE_ROWS - 1
+            ready = ahead_ref is not None and (tile + 1) * TILE_ROWS % stride == 0
+            held = index * (body_rows // stride) + tile * TILE_ROWS // stride
             for part, columns in enumerate(parts):
                 if ready:
-                    signs = ahead_ref[pl.ds(pl.multiple_of(index * depth, depth), depth), columns]
+                    signs = ahead_ref[pl.ds(pl.multiple_of(held * depth, depth), depth), columns]
                 else:
                     signs = sign_tile(base, row, columns, piece, half, place_ref)
                 sums[part] += jnp.dot(directed, signs, preferred_element_type=jnp.float32)
@@ -194,7 +195,7 @@
 
 
 def project(
-    place, seeds, received, moment_one, moment_two, before, ahead, sequences, piece, half, scale, body_rows
+    place, seeds, received, moment_one, moment_two, before, ahead, sequences, piece, half, scale, body_rows, stride
 ):
     rank = received.shape[1]
     features = seeds.shape[0] * FEAT_BLOCK
@@ -202,7 +203,7 @@
     whole = lambda array: pl.BlockSpec(array.shape, lambda block: (0, 0))
     part = pl.BlockSpec((sequences, FEAT_BLOCK), lambda block: (0, block))
     return pl.pallas_call(
-        functools.partial(project_kernel, (sequences, piece, half, rank, scale, body_rows)),
+        functools.partial(project_kernel, (sequences, piece, half, rank, scale, body_rows, stride)),
         grid=(seeds.shape[0],),
         in_specs=[
             pl.BlockSpec(memory_space=pltpu.SMEM),
@@ -317,7 +318,7 @@
         places.append(jnp.stack([in_slice, my_index * local_rows + in_slice]).astype(jnp.int32))
     partials = jnp.zeros((sequences, block_seeds.shape[0] * FEAT_BLOCK), jnp.float32)
     late_rows = 2 * pieces[1][1]
-    late_body = AHEAD_BODY if late_rows % AHEAD_BODY == 0 else math.gcd(late_rows, BODY_ROWS)
+    late_stride = AHEAD_STRIDE if late_rows % AHEAD_STRIDE == 0 else math.gcd(late_rows, BODY_ROWS)
     received = []
     ahead = []
     for chunk, (_, piece) in enumerate(pieces):
@@ -325,17 +326,17 @@
         summed = (blocks[chunk] + other).reshape(devices, piece, rank)
         if chunk == 0:
             late_place, summed = lax.optimization_barrier((places[1], summed))
-            ahead = [hash_ahead(late_place, block_seeds, pieces[1][1], half, rank, late_body)]
+            ahead = [hash_ahead(late_place, block_seeds, pieces[1][1], half, rank, late_stride)]
         else:
             summed, *ahead = lax.optimization_barrier((summed, *ahead))
         gathered = lax.all_to_all(summed, axes, split_axis=0, concat_axis=0, tiled=True)
         received.append(gathered.reshape(devices * piece, rank))
 
     for chunk, (_, piece) in enumerate(pieces):
-        body_rows = late_body if chunk else math.gcd(2 * piece, BODY_ROWS)
+        body_rows = math.gcd(2 * piece, 2 * late_stride if chunk else BODY_ROWS)
         partials = project(
             places[chunk], block_seeds, received[chunk], adam_first_moment, adam_second_moment, partials,
-            ahead if chunk else [], sequences, piece, half, scale, body_rows,
+            ahead if chunk else [], sequences, piece, half, scale, body_rows, late_stride,
         )
     shares = partials.reshape(devices, 8, -1)
     return sum_shares(shares, groups, device_list).reshape(1, -1)

time: 222 us -> 216 us (0.973)
  Pallas kernels: 193 us -> 190 us
    pallas_call x2, Pallas kernels: 164 us -> 157 us  [project(): pl.pallas_call(functools.partial(project_kernel, (sequences, piece, half,...]
    pallas_call x1, Pallas kernels: 4.78 us -> 7.78 us  [half_gradients(): pl.pallas_call(functools.partial(grad_kernel, (local_rows, groups, half,...]
where the time goes in v7:
time: 216 us
  Pallas kernels  190 us (88%)
  starting transfers between devices  11.8 us (5%)
  other arithmetic  6.69 us (3%)
  local copies, waits for them, and re-layouts  4.25 us (2%)
  waiting for transfers between devices  2.9 us (1%)
    pallas_call x2, Pallas kernels, project(): pl.pallas_call(functools.partial(project_kernel, (sequences, piece, half,...  157 us
    pallas_call x1, Pallas kernels, hash_ahead(): pl.pallas_call(functools.partial(ahead_kernel, (piece, half, body_rows)),...  12.7 us
    pallas_call x1, Pallas kernels, sum_shares(): pl.pallas_call(functools.partial(gather_kernel, groups, device_list), in_...  12.1 us
    all_to_all x2, starting transfers between devices, local(): lax.all_to_all(summed, axes, split_axis=0, concat_axis=0, tiled=True)  11.3 us
    pallas_call x1, Pallas kernels, half_gradients(): pl.pallas_call(functools.partial(grad_kernel, (local_rows, groups, half,...  7.78 us
  transfers between devices with their start and end apart: 4, of which 2 were waited for; matrix products, arithmetic and copies ran while one was open for 2% of the time, Pallas kernels for 25%

profile of v7, /device:TPU:0, one launch (start us, length us, event | category | flops | bytes accessed | tf_op | source)
XLA Modules:
  0.0 215.5 jit_solution(4123435962817597335)
XLA Ops:
  0.0 0.7 compare_convert_fusion
  0.7 1.6 broadcast_multiply_fusion.masked_ref
  2.2 7.8 %shard_map.64 = (f32[2,16,32,128]{3,2,1,0:T(8,128)}, f32[2,16,96,128]{3,2,1,0:T(8,128)}, f32[2,16,32,128]{3,2,1,0:T(8,128)}, f32[2,16,96,128]{3,2,1,0:T(8,128)}) custom-call(s32[1]{0:T(128)} %bitcast.2.side_ref, bf16[256,8192]{1,0:T(8,128)(2,1)} %hidden_ref.1, bf16[256,128]{1,0:T(8,128)(2,1)} %broadcast_multiply_fusion.masked_ref), custom_call_target="tpu_custom_call" | custom-call | flops 536870912 | bytes 8388608 | tf_op jit(solution)/shard_map/pallas_call | solution.py:61
  10.0 0.5 collective-permute-start.1
  10.5 0.1 collective-permute-start
  10.5 0.6 pad_add_fusion.place_ref
  11.1 1.1 collective-permute-done.1
  12.2 1.9 add.23
  14.1 7.2 %all-to-all-start.1 = ((f32[32,32,128]{2,1,0:T(8,128)}), f32[32,32,128]{2,1,0:T(8,128)S(1)}, u32[]{:S(2)}, u32[]{:S(2)}) async-start(f32[32,32,128]{2,1,0:T(8,128)} %bitcast.4), calls=%async_computation.1 | async-start | bytes 1048576 | tf_op jit(solution)/shard_map/all_to_all | solution.py:332
  21.4 0.0 copy-start.1
  21.4 12.7 %shard_map.65.refs_0_ = bf16[2048,4096]{1,0:T(8,128)(2,1)} custom-call(s32[2]{0:T(128)} %pad_add_fusion.place_ref, s32[8]{0:T(128)} %seeds_ref.5), custom_call_target="tpu_custom_call" | custom-call | flops 13421772800 | bytes 16777216 | tf_op jit(solution)/shard_map/pallas_call | solution.py:134
  34.1 0.0 collective-permute-done
  34.1 0.0 copy-done.1
  34.1 1.3 add.22
  35.5 1.8 all-to-all-done.1
  37.3 0.0 copy-start.2
  37.3 0.8 copy-done.2
  38.0 4.0 %all-to-all-start = ((f32[32,96,128]{2,1,0:T(8,128)}), f32[32,96,128]{2,1,0:T(8,128)S(1)}, u32[]{:S(2)}, u32[]{:S(2)}) async-start(f32[32,96,128]{2,1,0:T(8,128)} %bitcast.3), calls=%async_computation | async-start | bytes 3145728 | tf_op jit(solution)/shard_map/all_to_all | solution.py:332
  42.1 0.6 pad_add_fusion.1.place_ref
  42.7 0.7 broadcast_in_dim.4.before_ref
  43.4 41.8 %shard_map.66.before_ref = f32[16,4096]{1,0:T(8,128)} custom-call(s32[2]{0:T(128)} %pad_add_fusion.1.place_ref, s32[8]{0:T(128)} %seeds_ref.5, f32[1024,128]{1,0:T(8,128)} %bitcast.14, f32[512,128]{1,0:T(8,128)} %one_ref.3, f32[512,128]{1,0:T(8,128)} %two_ref.3, f32[16,4096]{1,0:T(8,128)} %broadcast_in_dim.4.before_ref), custom_call_target="tpu_custom_call" | custom-call | flops 13421772800 | bytes 524288 | tf_op jit(solution)/shard_map/pallas_call | solution.py:205
  85.2 0.0 all-to-all-done
  85.2 0.0 copy-start
  85.2 1.1 copy-done
  86.4 115.5 %shard_map.67 = f32[16,4096]{1,0:T(8,128)} custom-call(s32[2]{0:T(128)} %pad_add_fusion.place_ref, s32[8]{0:T(128)} %seeds_ref.5, f32[3072,128]{1,0:T(8,128)} %bitcast.13, f32[512,128]{1,0:T(8,128)} %one_ref.3, f32[512,128]{1,0:T(8,128)} %two_ref.3, f32[16,4096]{1,0:T(8,128)} %shard_map.66.before_ref, bf16[2048,4096]{1,0:T(8,128)(2,1)} %shard_map.65.refs_0_), custom_call_target="tpu_custom_call" | custom-call | flops 40265318400 | bytes 1572864 | tf_op jit(solution)/shard_map/pallas_call | solution.py:205
  201.9 1.0 reshape.27.shares_ref
  202.9 12.1 %shard_map.68 = f32[8,256]{1,0:T(8,128)S(1)} custom-call(f32[32,8,256]{2,1,0:T(8,128)S(1)} %reshape.27.shares_ref), custom_call_target="tpu_custom_call" | custom-call | flops 65536 | bytes 524288 | tf_op jit(solution)/shard_map/pallas_call | solution.py:268
  214.9 0.6 copy.7
Async XLA Ops:
  10.0 2.2 %collective-permute-start.1 = (f32[2,16,32,128]{3,2,1,0:T(8,128)}, f32[2,16,32,128]{3,2,1,0:T(8,128)S(1)}, u32[]{:S(2)}, u32[]{:S(2)}) collective-permute-start(f32[2,16,32,128]{3,2,1,0:T(8,128)} %get-tuple-element.16), channel_id=1, source_target_pairs={{0,1},{1,0},{2,3},{3,2},{4,5},{5,4},{6,7},{7,6},{8,9},{9,8},{10,11... | collective-permute-start | bytes 1572872 | tf_op jit(solution)/shard_map/ppermute | solution.py:325
  10.5 23.6 %collective-permute-start = (f32[2,16,96,128]{3,2,1,0:T(8,128)}, f32[2,16,96,128]{3,2,1,0:T(8,128)S(1)}, u32[]{:S(2)}, u32[]{:S(2)}) collective-permute-start(f32[2,16,96,128]{3,2,1,0:T(8,128)} %get-tuple-element.14), channel_id=1, source_target_pairs={{0,1},{1,0},{2,3},{3,2},{4,5},{5,4},{6,7},{7,6},{8,9},{9,8},{10,11... | collective-permute-start | bytes 4718600 | tf_op jit(solution)/shard_map/ppermute | solution.py:325
  14.1 23.1 %all-to-all-start.1 = ((f32[32,32,128]{2,1,0:T(8,128)}), f32[32,32,128]{2,1,0:T(8,128)S(1)}, u32[]{:S(2)}, u32[]{:S(2)}) async-start(f32[32,32,128]{2,1,0:T(8,128)} %bitcast.4), calls=%async_computation.1 | async-start | bytes 1048576 | tf_op jit(solution)/shard_map/all_to_all | solution.py:332
  21.4 12.8 %copy-start.1 = (f32[2,16,96,128]{3,2,1,0:T(8,128)S(1)}, f32[2,16,96,128]{3,2,1,0:T(8,128)}, u32[]{:S(2)}) copy-start(f32[2,16,96,128]{3,2,1,0:T(8,128)} %get-tuple-element.13) | copy-start | bytes 4718596
  37.3 0.8 copy-start.2
  38.0 47.2 %all-to-all-start = ((f32[32,96,128]{2,1,0:T(8,128)}), f32[32,96,128]{2,1,0:T(8,128)S(1)}, u32[]{:S(2)}, u32[]{:S(2)}) async-start(f32[32,96,128]{2,1,0:T(8,128)} %bitcast.3), calls=%async_computation | async-start | bytes 3145728 | tf_op jit(solution)/shard_map/all_to_all | solution.py:332
  85.2 1.2 copy-start

commit v8 on v7

--- a/solution.py
+++ b/solution.py
@@ -72,7 +72,7 @@
         out_shape=[
             jax.ShapeDtypeStruct((groups, device_list, size, rank), jnp.float32) for size in sizes
         ],
-        compiler_params=pltpu.CompilerParams(vmem_limit_bytes=60 * 2**20),
+        compiler_params=pltpu.CompilerParams(vmem_limit_bytes=32 * 2**20),
         cost_estimate=pl.CostEstimate(
             flops=2 * tokens * width * rank, bytes_accessed=2 * tokens * width + 4 * width * rank, transcendentals=0
         ),
@@ -333,7 +333,7 @@
         received.append(gathered.reshape(devices * piece, rank))
 
     for chunk, (_, piece) in enumerate(pieces):
-        body_rows = math.gcd(2 * piece, 2 * late_stride if chunk else BODY_ROWS)
+        body_rows = math.gcd(2 * piece, 4 * late_stride if chunk else BODY_ROWS)
         partials = project(
             places[chunk], block_seeds, received[chunk], adam_first_moment, adam_second_moment, partials,
             ahead if chunk else [], sequences, piece, half, scale, body_rows, late_stride,

time: 216 us -> 213 us (0.986)
  Pallas kernels: 190 us -> 184 us
  local copies, waits for them, and re-layouts: 4.25 us -> 6.43 us
    pallas_call x1, Pallas kernels: 7.78 us -> 4.78 us  [half_gradients(): pl.pallas_call(functools.partial(grad_kernel, (local_rows, groups, half,...]
    pallas_call x2, Pallas kernels: 157 us -> 155 us  [project(): pl.pallas_call(functools.partial(project_kernel, (sequences, piece, half,...]
    unnamed x7, local copies, waits for them, and re-layouts: 2.54 us -> 4.72 us
  transfers between devices with their start and end apart: 4 -> 4, of which waited for: 2 -> 2; matrix products, arithmetic and copies ran while one was open for 2% -> 3% of each run, Pallas kernels for 25% -> 26%
where the time goes in v8:
time: 213 us; the launch traced here: 212 us
  Pallas kernels  184 us (86%)
  starting transfers between devices  13.7 us (6%)
  other arithmetic  6.43 us (3%)
  local copies, waits for them, and re-layouts  6.43 us (3%)
    pallas_call x2, Pallas kernels, project(): pl.pallas_call(functools.partial(project_kernel, (sequences, piece, half,...  155 us
    all_to_all x2, starting transfers between devices, local(): lax.all_to_all(summed, axes, split_axis=0, concat_axis=0, tiled=True)  13.1 us
    pallas_call x1, Pallas kernels, hash_ahead(): pl.pallas_call(functools.partial(ahead_kernel, (piece, half, body_rows)),...  12.6 us
    pallas_call x1, Pallas kernels, sum_shares(): pl.pallas_call(functools.partial(gather_kernel, groups, device_list), in_...  11.9 us
    pallas_call x1, Pallas kernels, half_gradients(): pl.pallas_call(functools.partial(grad_kernel, (local_rows, groups, half,...  4.78 us
    unnamed x7, local copies, waits for them, and re-layouts  4.72 us
  transfers between devices with their start and end apart: 4, of which 2 were waited for; matrix products, arithmetic and copies ran while one was open for 3% of the time, Pallas kernels for 26%

profile of v8, /device:TPU:0, one launch (start us, length us, event | category | flops | bytes accessed | tf_op | source)
XLA Modules:
  0.0 212.2 jit_solution(6120309914969612030)
XLA Ops:
  0.0 0.7 compare_convert_fusion
  0.7 0.9 broadcast_multiply_fusion.masked_ref
  1.6 0.0 copy-start
  1.6 2.2 %copy-done = bf16[256,8192]{1,0:T(8,128)(2,1)S(1)} copy-done((bf16[256,8192]{1,0:T(8,128)(2,1)S(1)}, bf16[256,8192]{1,0:T(8,128)(2,1)}, u32[]{:S(2)}) %copy-start) | copy-done | bytes 4194328
  3.8 4.8 %shard_map.64 = (f32[2,16,32,128]{3,2,1,0:T(8,128)S(1)}, f32[2,16,96,128]{3,2,1,0:T(8,128)S(1)}, f32[2,16,32,128]{3,2,1,0:T(8,128)S(1)}, f32[2,16,96,128]{3,2,1,0:T(8,128)}) custom-call(s32[1]{0:T(128)} %bitcast.2.side_ref, bf16[256,8192]{1,0:T(8,128)(2,1)S(1)} %copy-done, bf16[256,128]{1,0:T(8,128)(2,1)S(1)} %broadcast_multiply_fusion.masked_ref), custom_call_target="tpu_custom_call" | custom-call | flops 536870912 | bytes 8388608 | tf_op jit(solution)/shard_map/pallas_call | solution.py:61
  8.6 0.5 collective-permute-start.1
  9.1 0.0 collective-permute-start
  9.1 0.6 pad_add_fusion.place_ref
  9.7 1.2 collective-permute-done.1
  10.9 0.9 add.23
  11.7 7.7 %all-to-all-start.1 = ((f32[32,32,128]{2,1,0:T(8,128)}), f32[32,32,128]{2,1,0:T(8,128)S(1)}, u32[]{:S(2)}, u32[]{:S(2)}) async-start(f32[32,32,128]{2,1,0:T(8,128)} %bitcast.4), calls=%async_computation.1 | async-start | bytes 1048576 | tf_op jit(solution)/shard_map/all_to_all | solution.py:332
  19.4 12.6 %shard_map.65.refs_0_ = bf16[2048,4096]{1,0:T(8,128)(2,1)} custom-call(s32[2]{0:T(128)} %pad_add_fusion.place_ref, s32[8]{0:T(128)} %seeds_ref.5), custom_call_target="tpu_custom_call" | custom-call | flops 13421772800 | bytes 16777216 | tf_op jit(solution)/shard_map/pallas_call | solution.py:134
  32.0 0.0 collective-permute-done
  32.0 2.8 %add.22 = f32[2,16,96,128]{3,2,1,0:T(8,128)} add(f32[2,16,96,128]{3,2,1,0:T(8,128)S(1)} %get-tuple-element.13, f32[2,16,96,128]{3,2,1,0:T(8,128)} %collective-permute-done) | non-fusion elementwise | flops 393216 | bytes 4718592 | tf_op jit(solution)/shard_map/add | solution.py:326
  34.8 0.5 all-to-all-done.1
  35.3 0.0 copy-start.2
  35.3 0.8 copy-done.2
  36.1 5.5 %all-to-all-start = ((f32[32,96,128]{2,1,0:T(8,128)}), f32[32,96,128]{2,1,0:T(8,128)S(1)}, u32[]{:S(2)}, u32[]{:S(2)}) async-start(f32[32,96,128]{2,1,0:T(8,128)} %bitcast.3), calls=%async_computation | async-start | bytes 3145728 | tf_op jit(solution)/shard_map/all_to_all | solution.py:332
  41.6 0.6 pad_add_fusion.1.place_ref
  42.2 0.7 broadcast_in_dim.4.before_ref
  42.9 41.8 %shard_map.66.before_ref = f32[16,4096]{1,0:T(8,128)} custom-call(s32[2]{0:T(128)} %pad_add_fusion.1.place_ref, s32[8]{0:T(128)} %seeds_ref.5, f32[1024,128]{1,0:T(8,128)} %bitcast.14, f32[512,128]{1,0:T(8,128)} %one_ref.3, f32[512,128]{1,0:T(8,128)} %two_ref.3, f32[16,4096]{1,0:T(8,128)} %broadcast_in_dim.4.before_ref), custom_call_target="tpu_custom_call" | custom-call | flops 13421772800 | bytes 524288 | tf_op jit(solution)/shard_map/pallas_call | solution.py:205
  84.7 0.0 all-to-all-done
  84.7 0.0 copy-start.1
  84.7 1.1 copy-done.1
  85.8 112.8 %shard_map.67 = f32[16,4096]{1,0:T(8,128)} custom-call(s32[2]{0:T(128)} %pad_add_fusion.place_ref, s32[8]{0:T(128)} %seeds_ref.5, f32[3072,128]{1,0:T(8,128)} %bitcast.13, f32[512,128]{1,0:T(8,128)} %one_ref.3, f32[512,128]{1,0:T(8,128)} %two_ref.3, f32[16,4096]{1,0:T(8,128)} %shard_map.66.before_ref, bf16[2048,4096]{1,0:T(8,128)(2,1)} %shard_map.65.refs_0_), custom_call_target="tpu_custom_call" | custom-call | flops 40265318400 | bytes 1572864 | tf_op jit(solution)/shard_map/pallas_call | solution.py:205
  198.7 1.0 reshape.27.shares_ref
  199.7 11.9 %shard_map.68 = f32[8,256]{1,0:T(8,128)S(1)} custom-call(f32[32,8,256]{2,1,0:T(8,128)S(1)} %reshape.27.shares_ref), custom_call_target="tpu_custom_call" | custom-call | flops 65536 | bytes 524288 | tf_op jit(solution)/shard_map/pallas_call | solution.py:268
  211.6 0.6 copy.7
Async XLA Ops:
  1.6 2.2 %copy-start = (bf16[256,8192]{1,0:T(8,128)(2,1)S(1)}, bf16[256,8192]{1,0:T(8,128)(2,1)}, u32[]{:S(2)}) copy-start(bf16[256,8192]{1,0:T(8,128)(2,1)} %hidden_ref.1) | copy-start | bytes 12582916
  8.6 2.3 %collective-permute-start.1 = (f32[2,16,32,128]{3,2,1,0:T(8,128)S(1)}, f32[2,16,32,128]{3,2,1,0:T(8,128)S(1)}, u32[]{:S(2)}, u32[]{:S(2)}) collective-permute-start(f32[2,16,32,128]{3,2,1,0:T(8,128)S(1)} %get-tuple-element.16), channel_id=1, source_target_pairs={{0,1},{1,0},{2,3},{3,2},{4,5},{5,4},{6,7},{7,6},{8,9},{9,8},{10,11... | collective-permute-start | bytes 1572872 | tf_op jit(solution)/shard_map/ppermute | solution.py:325
  9.1 23.0 %collective-permute-start = (f32[2,16,96,128]{3,2,1,0:T(8,128)}, f32[2,16,96,128]{3,2,1,0:T(8,128)}, u32[]{:S(2)}, u32[]{:S(2)}) collective-permute-start(f32[2,16,96,128]{3,2,1,0:T(8,128)} %get-tuple-element.14), channel_id=1, source_target_pairs={{0,1},{1,0},{2,3},{3,2},{4,5},{5,4},{6,7},{7,6},{8,9},{9,8},{10,11... | collective-permute-start | bytes 4718600 | tf_op jit(solution)/shard_map/ppermute | solution.py:325
  11.7 23.6 %all-to-all-start.1 = ((f32[32,32,128]{2,1,0:T(8,128)}), f32[32,32,128]{2,1,0:T(8,128)S(1)}, u32[]{:S(2)}, u32[]{:S(2)}) async-start(f32[32,32,128]{2,1,0:T(8,128)} %bitcast.4), calls=%async_computation.1 | async-start | bytes 1048576 | tf_op jit(solution)/shard_map/all_to_all | solution.py:332
  35.3 0.8 copy-start.2
  36.1 48.6 %all-to-all-start = ((f32[32,96,128]{2,1,0:T(8,128)}), f32[32,96,128]{2,1,0:T(8,128)S(1)}, u32[]{:S(2)}, u32[]{:S(2)}) async-start(f32[32,96,128]{2,1,0:T(8,128)} %bitcast.3), calls=%async_computation | async-start | bytes 3145728 | tf_op jit(solution)/shard_map/all_to_all | solution.py:332
  84.7 1.2 copy-start.1
